TPU v7x, 128 devices: a whole 4x4x4 slice. The times are simulated.
128 devices in a mesh: row: 4 (over z), col: 32 (over x, y, core).
Axes of the slice: x: 4, y: 4, z: 4, core: 2. Of those that a mesh axis runs over, the one named last changes fastest.
Arguments:
- image_features: float32 [16384, 1024], P(('row', 'col')), as said below
- text_features: float32 [16384, 1024], P(('col', 'row')), as said below
- logit_scale: float32 [1], replicated, may hold values from 4 to 4.6052
Outputs:
- mean_loss: float32 [1], replicated
- image_grad: float32 [16384, 1024], P(('row', 'col'))
- text_grad: float32 [16384, 1024], P(('col', 'row'))
- scale_grad: float32 [1], replicated
Inputs may be any that keep to these rules, and one draw needn't show every extreme that they name: `image_features`: rows of the features have norms between about 1 and 16. `text_features`: rows of the features have norms between about 1 and 16.
All inputs are finite; a program needn't handle non-finite values.
Results may differ from a plain program's by a relative error of at most 0.0035.
Values may be sent and summed in bfloat16 or wider, within the bound.
A program may use at most 128 MiB of HBM per device.

v0:
```python
import math

import jax
import jax.numpy as jnp
from jax import lax
from jax.sharding import PartitionSpec as P

EPS = 1e-06


def normalize(features):
    inverse = lax.rsqrt(jnp.sum(features * features, axis=1, keepdims=True) + EPS)
    return (features * inverse, inverse)


def contract_rows(left, right):
    return lax.dot_general(
        left, right, (((1,), (1,)), ((), ())), preferred_element_type=jnp.float32
    )


def local(image_features, text_features, logit_scale):
    own_rows = image_features.shape[0]
    width = image_features.shape[1]
    row_count = lax.axis_size("row")
    col_count = lax.axis_size("col")
    row_index = lax.axis_index("row")
    col_index = lax.axis_index("col")
    image_hat, image_inv = normalize(image_features)
    text_hat, text_inv = normalize(text_features)
    image_rows = lax.all_gather(image_hat.astype(jnp.bfloat16), "col", axis=0, tiled=True)
    text_cols = lax.all_gather(text_hat.astype(jnp.bfloat16), "row", axis=0, tiled=True)
    tile_rows = image_rows.shape[0]
    tile_cols = text_cols.shape[0]
    block = math.gcd(tile_rows, 512)
    steps = tile_rows // block
    scale = jnp.exp(logit_scale[0])
    row_base = row_index * tile_rows
    col_ids = col_index * tile_cols + lax.broadcasted_iota(jnp.int32, (1, tile_cols), 1)
    image_blocks = image_rows.reshape(steps, block, width)
    starts = jnp.arange(steps, dtype=jnp.int32) * block

    def scores_of(rows, start):
        values = scale * contract_rows(rows, text_cols)
        row_ids = row_base + start + lax.broadcasted_iota(jnp.int32, (block, 1), 0)
        return (values, row_ids == col_ids)

    def forward(carry, item):
        col_peak, col_total, diag_sum = carry
        rows, start = item
        values, same = scores_of(rows, start)
        row_peak = jnp.max(values, axis=1)
        row_total = jnp.sum(jnp.exp(values - row_peak[:, None]), axis=1)
        peak = jnp.maximum(col_peak, jnp.max(values, axis=0))
        col_total = col_total * jnp.exp(col_peak - peak) + jnp.sum(
            jnp.exp(values - peak[None, :]), axis=0
        )
        diag_sum = diag_sum + jnp.sum(jnp.where(same, values, 0.0))
        return ((peak, col_total, diag_sum), (row_peak, row_total))

    init = (
        jnp.full((tile_cols,), -jnp.inf, jnp.float32),
        jnp.zeros((tile_cols,), jnp.float32),
        jnp.zeros((), jnp.float32),
    )
    (col_peak, col_total, diag_sum), (row_peak, row_total) = lax.scan(
        forward, init, (image_blocks, starts)
    )
    row_peak = row_peak.reshape(tile_rows)
    row_total = row_total.reshape(tile_rows)
    row_top = lax.pmax(row_peak, "col")
    row_total = lax.psum(row_total * jnp.exp(row_peak - row_top), "col")
    row_peak = row_top
    col_top = lax.pmax(col_peak, "row")
    col_total = lax.psum(col_total * jnp.exp(col_peak - col_top), "row")
    col_peak = col_top
    row_lse = row_peak + jnp.log(row_total)
    col_lse = col_peak + jnp.log(col_total)

    def backward(carry, item):
        text_sum, scale_sum = carry
        rows, start, lse_block = item
        values, same = scores_of(rows, start)
        probs = 0.5 * (jnp.exp(values - lse_block[:, None]) + jnp.exp(values - col_lse[None, :]))
        grad = probs - same.astype(jnp.float32)
        grad_low = grad.astype(jnp.bfloat16)
        text_part = lax.dot_general(
            grad_low, rows, (((0,), (0,)), ((), ())), preferred_element_type=jnp.float32
        )
        return ((text_sum + text_part, scale_sum + jnp.sum(grad * values)), grad_low)

    init_back = (jnp.zeros((tile_cols, width), jnp.float32), jnp.zeros((), jnp.float32))
    (text_sum, scale_sum), grad_blocks = lax.scan(
        backward, init_back, (image_blocks, starts, row_lse.reshape(steps, block))
    )
    grad_tile = grad_blocks.reshape(tile_rows, tile_cols)
    image_hat_grad = lax.psum_scatter(
        scale * jnp.dot(grad_tile, text_cols, preferred_element_type=jnp.float32),
        "col",
        scatter_dimension=0,
        tiled=True,
    )
    text_hat_grad = lax.psum_scatter(scale * text_sum, "row", scatter_dimension=0, tiled=True)
    own_row_lse = lax.dynamic_slice_in_dim(row_lse, col_index * own_rows, own_rows)
    own_col_lse = lax.dynamic_slice_in_dim(col_lse, row_index * own_rows, own_rows)
    loss_part = jnp.sum(own_row_lse) + jnp.sum(own_col_lse) - 2.0 * diag_sum
    total_loss, total_scale = lax.psum((loss_part, scale_sum), ("row", "col"))
    pairs = own_rows * row_count * col_count
    mean_loss = (total_loss / (2.0 * pairs)).reshape(1)
    scale_grad = (total_scale / pairs).reshape(1)
    image_grad = image_inv * (
        image_hat_grad - image_hat * jnp.sum(image_hat * image_hat_grad, axis=1, keepdims=True)
    )
    text_grad = text_inv * (
        text_hat_grad - text_hat * jnp.sum(text_hat * text_hat_grad, axis=1, keepdims=True)
    )
    return (mean_loss, image_grad, text_grad, scale_grad)


def solution(mesh):
    in_specs = (P(("row", "col"), None), P(("col", "row"), None), P())
    out_specs = (P(), P(("row", "col"), None), P(("col", "row"), None), P())
    return jax.shard_map(local, mesh=mesh, in_specs=in_specs, out_specs=out_specs, check_vma=False)
```

profile of v0, /device:TPU:1, one launch (start us, length us, event | category | flops | bytes accessed | tf_op | source)
XLA Modules:
  0.0 636.3 jit_solution(3943524549869024448)
XLA Ops:
  14.2 22.7 %all-gather.5.cloned.1.call-done = bf16[512,1024]{1,0:T(8,128)(2,1)} async-done(((bf16[128,1024]{1,0:T(8,128)(2,1)}), bf16[512,1024]{1,0:T(8,128)(2,1)}) %all-gather.5.cloned.1.call-update) | async-done | bytes 1048592 | tf_op jit(solution)/shard_map/all_gather | solution.py:32
  36.9 57.4 %all-gather.3.cloned.1.call-done = bf16[4096,1024]{1,0:T(8,128)(2,1)} async-done(((bf16[128,1024]{1,0:T(8,128)(2,1)}), bf16[4096,1024]{1,0:T(8,128)(2,1)}) %all-gather.3.cloned.1.call-update) | async-done | bytes 8388624 | tf_op jit(solution)/shard_map/all_gather | solution.py:31
  94.3 44.6 %while.34 = (s32[]{:T(128)}, f32[512]{0:T(512)S(1)}, f32[512]{0:T(512)S(1)}, f32[]{:T(128)}, f32[8,512]{1,0:T(8,128)S(1)}, /*index=5*/f32[8,512]{1,0:T(8,128)S(1...) while((s32[]{:T(128)}, f32[512]{0:T(512)S(1)}, ...), condition=%wide.region_8.9_spmd.clone, body=%wide.region_2.8_spmd.clone.sunk | while | flops 539494912 | bytes 4244180 | solution.py:66
  138.9 8.7 %pmax.15 = f32[512]{0:T(512)S(1)} all-reduce(f32[512]{0:T(512)S(1)} %get-tuple-element.136), channel_id=1, replica_groups=mesh['row'=4,'col'=32] {'row'}, use_global_device_ids=true, to_apply=%region_12.13 | all-reduce | flops 512 | bytes 4096 | tf_op jit(solution)/shard_map/pmax | solution.py:74
  147.5 6.0 psum.29
  153.5 122.1 %pmax.14 = f32[4096]{0:T(1024)S(1)} all-reduce(f32[4096]{0:T(1024)S(1)} %bitcast.70), channel_id=1, replica_groups=mesh['row'=4,'col'=32] {'col'}, use_global_device_ids=true, to_apply=%region_9.10 | all-reduce | flops 4096 | bytes 32768 | tf_op jit(solution)/shard_map/pmax | solution.py:71
  275.7 123.8 %psum.28 = f32[4096]{0:T(1024)S(1)} all-reduce(f32[4096]{0:T(1024)S(1)} %exponential_multiply_fusion), channel_id=1, replica_groups=mesh['row'=4,'col'=32] {'col'}, use_global_device_ids=true, to_apply=%region_10.11 | all-reduce | flops 4096 | bytes 32768 | tf_op jit(solution)/shard_map/psum | solution.py:72
  399.5 74.7 %while.35 = (s32[]{:T(128)}, f32[512,1024]{1,0:T(8,128)S(1)}, f32[]{:T(128)}, bf16[8,512,512]{2,1,0:T(8,128)(2,1)}, f32[]{:T(128)}, /*index=5*/bf16[8,512,1024]{...) while((s32[]{:T(128)}, f32[512,1024]{1,0:T(8,128)S(1)}, ...), condition=%wide.region_18.19_spmd.clone, body=%wide.region_16.18_spmd.clone.sunk | while | flops 1081607168 | bytes 11043543 | solution.py:93
  400.8 3.3 multiply_reduce_fusion.6
  404.7 2.8 select_add_fusion.2
  410.1 3.3 multiply_reduce_fusion.6
  419.4 3.3 multiply_reduce_fusion.6
  428.8 3.3 multiply_reduce_fusion.6
  432.7 2.8 select_add_fusion.2
  438.1 3.3 multiply_reduce_fusion.6
  442.1 2.8 select_add_fusion.2
  447.4 3.3 multiply_reduce_fusion.6
  451.4 2.8 select_add_fusion.2
  456.8 3.3 multiply_reduce_fusion.6
  466.1 3.3 multiply_reduce_fusion.6
  470.1 2.8 select_add_fusion.2
  475.7 10.6 %broadcast_multiply_fusion = f32[4096,1024]{1,0:T(8,128)} fusion(f32[]{:T(128)} %bitcast, bf16[4096,512]{1,0:T(8,128)(2,1)} %bitcast.75, bf16[512,1024]{1,0:T(8,128)(2,1)S(1)} %copy-done.2), kind=kOutput, calls=%fused_computation.29 | convolution fusion | flops 4299161600 | bytes 22020100 | tf_op jit(solution)/shard_map/dot_general | solution.py:98
  489.0 68.1 %all-reduce = (f32[]{:T(128)}, f32[]{:T(128)}) all-reduce(f32[]{:T(128)S(6)} %sub.57, f32[]{:T(128)} %get-tuple-element.141), channel_id=1, replica_groups=mesh['row'=4,'col'=32] {'row','col'}, use_global_device_ids=true, to_apply=%region_15.16 | all-reduce | flops 2 | bytes 16 | tf_op jit(solution)/shard_map/psum | solution.py:107
  561.8 62.5 %reduce-scatter.3.cloned.1.call-done = f32[128,1024]{1,0:T(8,128)} async-done(((f32[4096,1024]{1,0:T(8,128)}), f32[128,1024]{1,0:T(8,128)}) %reduce-scatter.3.cloned.1.call-update) | async-done | bytes 524304 | tf_op jit(solution)/shard_map/reduce_scatter | solution.py:97
  (165 shorter events, 72.8 us)
Async XLA Ops:
  7.2 29.7 %all-gather.5.cloned.1.call-start = ((), (), s32[]{:S(2)}) async-start(), calls=%async_computation.3 | async-start | bytes 1310720 | tf_op jit(solution)/shard_map/all_gather | solution.py:32
  10.3 84.0 %all-gather.3.cloned.1.call-start = ((), (), s32[]{:S(2)}) async-start(), calls=%async_computation.2 | async-start | bytes 8650752 | tf_op jit(solution)/shard_map/all_gather | solution.py:31
  13.3 545.2 %reduce-scatter.5.cloned.1.call-start = ((), (), s32[]{:S(2)}) async-start(), calls=%async_computation.5 | async-start | bytes 2621440 | tf_op jit(solution)/shard_map/reduce_scatter | solution.py:103
  474.2 1.6 copy-start.2
  475.7 148.6 %reduce-scatter.3.cloned.1.call-start = ((), (), s32[]{:S(2)}) async-start(), calls=%async_computation.4 | async-start | bytes 17301504 | tf_op jit(solution)/shard_map/reduce_scatter | solution.py:97
  486.4 72.2 %copy-start = (f32[128,1024]{1,0:T(8,128)S(1)}, f32[128,1024]{1,0:T(8,128)}, u32[]{:S(2)}) copy-start(f32[128,1024]{1,0:T(8,128)} %param.8) | copy-start | bytes 1572868
  486.4 137.9 %copy-start.1 = (f32[128,1024]{1,0:T(8,128)S(1)}, f32[128,1024]{1,0:T(8,128)}, u32[]{:S(2)}) copy-start(f32[128,1024]{1,0:T(8,128)} %param.7) | copy-start | bytes 1572868
Sparse Core Ops, SparseCore 0:
  10.4 26.4 all-gather.4
  39.7 54.4 all-gather.2
  475.8 30.4 reduce-scatter.4
  510.6 113.6 reduce-scatter.2
where the time goes:
time: 639 us; the launch traced here: 636 us
  blocking collectives  329 us (51%)
  waiting for transfers between devices  143 us (22%)
  matrix products  78.6 us (12%)
  other arithmetic  34.7 us (5%)
  loops' own time  21.6 us (3%)
  between operations  19.4 us (3%)
  local copies, waits for them, and re-layouts  10.5 us (2%)
    psum x1, blocking collectives, local(): row_total = lax.psum(row_total * jnp.exp(row_peak - row_top), 'col')  124 us
    pmax x1, blocking collectives, local(): row_top = lax.pmax(row_peak, 'col')  122 us
    psum x1, blocking collectives, local(): total_loss, total_scale = lax.psum((loss_part, scale_sum), ('row', 'col'))  68.1 us
    reduce_scatter x1, waiting for transfers between devices, local(): lax.psum_scatter(scale * jnp.dot(grad_tile, text_cols, preferred_element_...  62.5 us
    all_gather x1, waiting for transfers between devices, local(): lax.all_gather(image_hat.astype(jnp.bfloat16), 'col', axis=0, tiled=True)  57.4 us
    dot_general x16, matrix products, contract_rows(): lax.dot_general(left, right, (((1,), (1,)), ((), ())), preferred_element_...  45.4 us
    all_gather x1, waiting for transfers between devices, local(): lax.all_gather(text_hat.astype(jnp.bfloat16), 'row', axis=0, tiled=True)  22.7 us
    dot_general x8, matrix products, backward(): lax.dot_general(grad_low, rows, (((0,), (0,)), ((), ())), preferred_eleme...  22.5 us
  transfers between devices with their start and end apart: 4, of which 3 were waited for; matrix products, arithmetic and copies ran while one was open for 3% of the time, Pallas kernels for 0%

commit v1 on v0

v1 whole, which is shorter than its diff:
```python
import functools

import jax
import jax.numpy as jnp
from jax import lax
from jax.experimental import pallas as pl
from jax.experimental.pallas import tpu as pltpu
from jax.sharding import PartitionSpec as P

MESH = pl.DeviceIdType.MESH
EPS = 1e-06
LOG2E = 1.4426950408889634
LN2 = 0.6931471805599453
SHIFT = 34.0
TINY = 2.0**-60

CHUNK = 128
WIDTH = 1024
ORDER = (0, 1, 2, 4, 3, 5, 6, 7)
RANK = tuple(ORDER.index(q) for q in range(8))
PARTS = ((0, 48), (48, 48), (96, 32))
BF16 = jnp.bfloat16
F32 = jnp.float32


def stage_dim(part, stage):
    return (part + stage) % 3


def last_stage(q, part):
    stage = -1
    for t in range(3):
        if q >> stage_dim(part, t) & 1:
            stage = t
    return stage


def log2(x):
    return jnp.log(x) * LOG2E


def nt(a, b):
    return lax.dot_general(a, b, (((1,), (1,)), ((), ())), preferred_element_type=F32)


def nn(a, b):
    return lax.dot_general(a, b, (((1,), (0,)), ((), ())), preferred_element_type=F32)


def tn(a, b):
    return lax.dot_general(a, b, (((0,), (0,)), ((), ())), preferred_element_type=F32)


def flip_image(c):
    return c + 1 - 2 * lax.rem(c, 2)


def flip_text(c):
    return 3 - c


def kernel(
    scale_ref, image_ref, text_ref,
    image_out, text_out, sums_out,
    img, txt, u_s, grad_s, hi_s, lo_s, colhi_s, collo_s,
    rowl_s, rowl_r, coll_s, coll_r, rlse_s, clse_s, crow_s,
    a_img, a_txt, core_s, core_r, rs_s, rs_r,
    part_s, part_r, part2_s, part2_r,
    ag_send, ag_recv, core_send, core_recv,
    lse_send, lse_recv, csum_send, csum_recv, rs_send, rs_recv, tot_send, tot_recv,
):
    z = lax.axis_index("row")
    c = lax.axis_index("col")
    x, y, k = c // 8, lax.rem(c // 2, 4), lax.rem(c, 2)
    at = (x, y, z)
    flipped = (tuple(flip_image(v) for v in at), tuple(flip_text(v) for v in at))

    def place(side, q, other_core=0):
        px, py, pz = (flipped[side][d] if q >> d & 1 else at[d] for d in range(3))
        return {"row": pz, "col": (px * 4 + py) * 2 + (1 - k if other_core else k)}

    def remote(src, dst, send, recv, device):
        return pltpu.make_async_remote_copy(
            src_ref=src, dst_ref=dst, send_sem=send, recv_sem=recv, device_id=device, device_id_type=MESH
        )

    peers = [place(0, j >> 1, j & 1) for j in range(1, 16)] + [place(1, q) for q in range(1, 8)]
    barrier = pltpu.get_barrier_semaphore()
    for peer in peers:
        pl.semaphore_signal(barrier, inc=1, device_id=peer, device_id_type=MESH)

    def normalized(ref):
        v = ref[...]
        inverse = lax.rsqrt(jnp.sum(v * v, axis=1, keepdims=True) + EPS)
        return v * inverse, inverse

    img[pl.ds(0, CHUNK), :] = normalized(image_ref)[0].astype(BF16)
    txt[pl.ds(0, CHUNK), :] = normalized(text_ref)[0].astype(BF16)
    scale = jnp.exp(jnp.full((8, 128), scale_ref[0], F32))[0:1, 0:1]
    unit = scale * LOG2E
    hi_s[...] = jnp.zeros_like(hi_s)
    lo_s[...] = jnp.zeros_like(lo_s)
    colhi_s[...] = jnp.zeros_like(colhi_s)
    collo_s[...] = jnp.zeros_like(collo_s)

    pl.semaphore_wait(barrier, len(peers))

    def gather_rows(side, q, part):
        start, rows = PARTS[part]
        base = RANK[q] * (2 * CHUNK if side == 0 else CHUNK)
        return (img, txt)[side].at[pl.ds(base + start, rows)]

    def gather_copy(side, q, part):
        d = stage_dim(part, last_stage(q, part))
        i = (q - 1) * 3 + part
        return remote(
            gather_rows(side, q ^ (1 << d), part), gather_rows(side, q, part),
            ag_send.at[side, i], ag_recv.at[side, i], place(side, 1 << d),
        )

    def core_copy(q, part):
        start, rows = PARTS[part]
        base = RANK[q] * 2 * CHUNK + start
        return remote(
            img.at[pl.ds(base, rows)], img.at[pl.ds(base + CHUNK, rows)],
            core_send.at[q * 3 + part], core_recv.at[q * 3 + part], place(0, 0, 1),
        )

    def arrive(q, part, sides=(0, 1)):
        for side in sides:
            gather_copy(side, q, part).wait_recv()
            for t in range(last_stage(q, part) + 1, 3):
                gather_copy(side, q | 1 << stage_dim(part, t), part).start()
            if side == 0:
                core_copy(q, part).start()

    for t in range(3):
        for d in range(3):
            for side in range(2):
                gather_copy(side, 1 << d, (d - t) % 3).start()
    for part in range(3):
        core_copy(0, part).start()

    def scores(row0, rows, col0, cols):
        def block(i, _):
            r = pl.multiple_of(row0 + i * 256, 256)
            u = nt(img[pl.ds(r, 256), :], txt[pl.ds(col0, cols), :]) * unit
            u_s[pl.ds(r, 256), pl.ds(col0, cols)] = u
            hi = jnp.exp2(u - SHIFT)
            lo = jnp.exp2(jnp.minimum(u, 0.0) + SHIFT)
            for e, row_s, col_s in ((hi, hi_s, colhi_s), (lo, lo_s, collo_s)):
                row = e[:, 0:128]
                for j in range(1, cols // 128):
                    row = row + e[:, j * 128 : (j + 1) * 128]
                row_s[pl.ds(r, 256), :] += row
                col_s[:, pl.ds(col0, cols)] += jnp.sum(e.reshape(32, 8, cols), axis=0)
            return 0

        lax.fori_loop(0, rows // 256, block, 0)

    for part in range(3):
        arrive(1 << part, part)
    for d in range(3):
        arrive(1 << d, (d - 1) % 3)
    for d in range(3):
        arrive(1 << d, (d - 2) % 3)
    for q in (0, 1, 2, 4):
        for part in range(3):
            core_copy(q, part).wait_recv()
    scores(0, 1024, 0, 512)
    for d in range(3):
        arrive(1 << d | 1 << (d - 1) % 3, (d - 1) % 3)
    for d in range(3):
        arrive(1 << d | 1 << (d - 2) % 3, (d - 2) % 3)
    for d in range(3):
        arrive(1 << d | 1 << (d - 1) % 3, (d - 2) % 3)
    for q in (3, 5, 6):
        for part in range(3):
            core_copy(q, part).wait_recv()
    scores(0, 1792, 512, 256)
    scores(1024, 768, 0, 512)
    for d in range(3):
        arrive(7, (d - 2) % 3)
    for part in range(3):
        core_copy(7, part).wait_recv()
    scores(0, 2048, 768, 256)
    scores(1792, 256, 0, 768)

    def joined(hi, lo):
        return jnp.where(hi > TINY, log2(hi) + SHIFT, log2(lo) - SHIFT)

    def absolute(side, q):
        bits = [lax.rem(v, 2) for v in at] if side == 0 else [v // 2 for v in at]
        bits = [1 - b if q >> d & 1 else b for d, b in enumerate(bits)]
        return bits[0] + 2 * bits[1] + 4 * bits[2]

    def row_index(q, other):
        return absolute(0, q) * 2 + (1 - k if other else k)

    for q in range(8):
        for other in range(2):
            r = RANK[q] * 256 + other * CHUNK
            hi = jnp.sum(hi_s[pl.ds(r, CHUNK), :].T, axis=0, keepdims=True)
            lo = jnp.sum(lo_s[pl.ds(r, CHUNK), :].T, axis=0, keepdims=True)
            rowl_s[pl.ds(row_index(q, other), 1), :] = joined(hi, lo)
    colsum = joined(
        jnp.sum(colhi_s[...], axis=0, keepdims=True), jnp.sum(collo_s[...], axis=0, keepdims=True)
    )
    for q in range(8):
        coll_s[pl.ds(absolute(1, q), 1), :] = colsum[:, RANK[q] * 128 : (RANK[q] + 1) * 128]

    def row_copy(j):
        return remote(rowl_s, rowl_r.at[j - 1], lse_send.at[j - 1], lse_recv.at[j - 1], place(0, j >> 1, j & 1))

    def col_copy(q):
        return remote(coll_s, coll_r.at[q - 1], csum_send.at[q - 1], csum_recv.at[q - 1], place(1, q))

    for q in range(1, 8):
        col_copy(q).start()
    for j in range(1, 16):
        row_copy(j).start()
    for q in range(1, 8):
        col_copy(q).wait_recv()
    for j in range(1, 16):
        row_copy(j).wait_recv()

    def over(values):
        top = functools.reduce(jnp.maximum, values)
        return top + log2(functools.reduce(jnp.add, [jnp.exp2(v - top) for v in values]))

    rlse_s[...] = over([rowl_s[...]] + [rowl_r[j] for j in range(15)])
    clse_s[...] = over([coll_s[...]] + [coll_r[j] for j in range(7)])
    for q in range(8):
        crow_s[:, pl.ds(RANK[q] * 128, 128)] = clse_s[pl.ds(absolute(1, q), 1), :] + 1.0

    eye = (
        lax.broadcasted_iota(jnp.int32, (CHUNK, CHUNK), 0) == lax.broadcasted_iota(jnp.int32, (CHUNK, CHUNK), 1)
    )
    part_s[...] = jnp.zeros_like(part_s)

    def diagonal_slot(q, other):
        ix, iy, iz = (flipped[0][d] if q >> d & 1 else at[d] for d in range(3))
        ik = 1 - k if other else k
        tx, ty, tk, tz = iz, ix, iy // 2, lax.rem(iy, 2) * 2 + ik
        here = tk == k
        rank = 0
        for d, t in enumerate((tx, ty, tz)):
            across = t == flipped[1][d]
            here = here & (across | (t == at[d]))
            rank = rank + jnp.where(across, 1 << d, 0)
        rank = jnp.where(rank == 3, 4, jnp.where(rank == 4, 3, rank))
        return here, rank

    def column(row):
        return jnp.broadcast_to(row, (CHUNK, CHUNK)).T

    def grads(q, other):
        r = RANK[q] * 256 + other * CHUNK
        lse = column(rlse_s[pl.ds(row_index(q, other), 1), :] + 1.0)
        total = jnp.zeros((8, 128), F32)
        for j in range(8):
            u = u_s[pl.ds(r, CHUNK), pl.ds(j * 128, 128)]
            g = jnp.exp2(u - lse) + jnp.exp2(u - crow_s[:, pl.ds(j * 128, 128)])
            grad_s[pl.ds(r, CHUNK), pl.ds(j * 128, 128)] = g.astype(BF16)
            total = total + jnp.sum((g * u).reshape(16, 8, 128), axis=0)
        part_s[pl.ds(8, 8), :] += total
        here, rank = diagonal_slot(q, other)

        @pl.when(here)
        def _():
            at_col = pl.ds(pl.multiple_of(rank * 128, 128), 128)
            u = u_s[pl.ds(r, CHUNK), at_col]
            g = jnp.exp2(u - lse) + jnp.exp2(u - crow_s[:, at_col])
            grad_s[pl.ds(r, CHUNK), at_col] = jnp.where(eye, g - 1.0, g).astype(BF16)
            part_s[pl.ds(0, 8), :] += jnp.sum(jnp.where(eye, u, 0.0).reshape(16, 8, 128), axis=0)

    for q in range(8):
        for other in range(2):
            grads(q, other)
    diagonal = part_s[pl.ds(0, 8), :]
    part_s[pl.ds(8, 8), :] += -diagonal
    part_s[pl.ds(0, 8), :] = -2.0 * diagonal
    part_s[pl.ds(0, 1), :] += rlse_s[pl.ds(row_index(0, 0), 1), :] + clse_s[pl.ds(absolute(1, 0), 1), :]

    def total_copy(stage, j):
        if stage == 0:
            src, dst, device = part_s, part_r, place(0, j >> 1, j & 1)
        else:
            src, dst, device = part2_s, part2_r, place(1, j)
        i = j - 1 + 15 * stage
        return remote(src, dst.at[j - 1], tot_send.at[i], tot_recv.at[i], device)

    for j in range(1, 16):
        total_copy(0, j).start()

    def image_product(q):
        r = RANK[q] * 256
        for n in range(0, WIDTH, 256):
            acc = nn(grad_s[pl.ds(r, 256), :], txt[:, pl.ds(n, 256)])
            a_img[pl.ds(RANK[q] * CHUNK, CHUNK), pl.ds(n, 256)] = acc[0:CHUNK]
            core_s[pl.ds(q * CHUNK, CHUNK), pl.ds(n, 256)] = acc[CHUNK:].astype(BF16)
        sibling(q).start()

    def sibling(q):
        here = pl.ds(q * CHUNK, CHUNK)
        return remote(core_s.at[here], core_r.at[here], core_send.at[24 + q], core_recv.at[24 + q], place(0, 0, 1))

    def join_cores(q):
        sibling(q).wait_recv()
        here = pl.ds(RANK[q] * CHUNK, CHUNK)
        a_img[here, :] += core_r[pl.ds(q * CHUNK, CHUNK), :].astype(F32)

    def text_product(pair):
        for n in range(0, WIDTH, 256):
            acc = tn(grad_s[:, pl.ds(pair * 256, 256)], img[:, pl.ds(n, 256)])
            a_txt[pl.ds(pair * 256, 256), pl.ds(n, 256)] = acc

    def region(q, part, stage):
        kept = [p for p in range(8) if all(not p >> stage_dim(part, t) & 1 for t in range(stage, 3))]
        return {2: 0, 1: 4, 0: 6}[stage] + kept.index(q)

    def sum_copy(side, q, part):
        stage = last_stage(q, part)
        d = stage_dim(part, stage)
        start, rows = PARTS[part]
        to = region(q ^ (1 << d), part, stage)
        i = to * 3 + part
        return remote(
            rs_s.at[side, pl.ds(q * CHUNK + start, rows)], rs_r.at[side, pl.ds(to * CHUNK + start, rows)],
            rs_send.at[side, i], rs_recv.at[side, i], place(side, 1 << d),
        )

    def summed(side, q, part):
        start, rows = PARTS[part]
        acc = (a_img, a_txt)[side][pl.ds(RANK[q] * CHUNK + start, rows), :]
        for stage in range(2, last_stage(q, part), -1):
            d = stage_dim(part, stage)
            sum_copy(side, q | 1 << d, part).wait_recv()
            acc = acc + rs_r[side, pl.ds(region(q, part, stage) * CHUNK + start, rows), :].astype(F32)
        return acc

    def hand_on(side, q, part):
        start, rows = PARTS[part]
        rs_s[side, pl.ds(q * CHUNK + start, rows), :] = summed(side, q, part).astype(BF16)
        sum_copy(side, q, part).start()

    def rounds(side, slots, age):
        for q in slots:
            for part in range(3):
                if 2 - last_stage(q, part) == age:
                    hand_on(side, q, part)

    image_product(7)
    text_product(3)
    join_cores(7)
    rounds(0, (7,), 0)
    rounds(1, (7,), 0)
    rounds(1, (6,), 0)
    image_product(6)
    image_product(5)
    join_cores(6)
    rounds(0, (6,), 0)
    text_product(2)
    rounds(1, (5, 3), 0)
    join_cores(5)
    rounds(0, (5,), 0)
    image_product(3)
    image_product(4)
    join_cores(3)
    rounds(0, (3,), 0)
    rounds(0, (6, 5, 3), 1)
    rounds(1, (6, 5, 3), 1)
    join_cores(4)
    rounds(0, (4,), 0)
    text_product(1)
    rounds(1, (4, 2), 0)
    image_product(2)
    image_product(1)
    join_cores(2)
    rounds(0, (2,), 0)
    text_product(0)
    rounds(1, (1,), 0)
    join_cores(1)
    rounds(0, (1,), 0)
    rounds(0, (4, 2, 1), 1)
    rounds(1, (4, 2, 1), 1)
    image_product(0)
    for j in range(1, 16):
        total_copy(0, j).wait_recv()
    part2_s[...] = functools.reduce(jnp.add, [part_s[...]] + [part_r[j] for j in range(15)])
    for q in range(1, 8):
        total_copy(1, q).start()
    rounds(0, (4, 2, 1), 2)
    rounds(1, (4, 2, 1), 2)
    join_cores(0)

    for side, ref, out in ((0, image_ref, image_out), (1, text_ref, text_out)):
        for part, (start, rows) in enumerate(PARTS):
            here = pl.ds(start, rows)
            v = ref[here, :]
            inverse = lax.rsqrt(jnp.sum(v * v, axis=1, keepdims=True) + EPS)
            hat = v * inverse
            g = summed(side, 0, part) * scale
            out[here, :] = inverse * (g - hat * jnp.sum(hat * g, axis=1, keepdims=True))

    for q in range(1, 8):
        total_copy(1, q).wait_recv()
    totals = functools.reduce(jnp.add, [part2_s[...]] + [part2_r[j] for j in range(7)])
    pairs = 128.0 * CHUNK
    sums_out[0] = jnp.sum(totals[0:8]) * (LN2 / (2.0 * pairs))
    sums_out[1] = jnp.sum(totals[8:16]) * (LN2 / pairs)

    for side in range(2):
        for q in range(1, 8):
            for part in range(3):
                gather_copy(side, q, part).wait_send()
                sum_copy(side, q, part).wait_send()
    for q in range(8):
        sibling(q).wait_send()
        for part in range(3):
            core_copy(q, part).wait_send()
    for j in range(1, 16):
        row_copy(j).wait_send()
        total_copy(0, j).wait_send()
    for q in range(1, 8):
        col_copy(q).wait_send()
        total_copy(1, q).wait_send()


def local(image_features, text_features, logit_scale):
    vmem = pl.BlockSpec(memory_space=pltpu.VMEM)
    smem = pl.BlockSpec(memory_space=pltpu.SMEM)
    dma = pltpu.SemaphoreType.DMA
    image_grad, text_grad, sums = pl.pallas_call(
        kernel,
        out_shape=(
            jax.ShapeDtypeStruct((CHUNK, WIDTH), F32),
            jax.ShapeDtypeStruct((CHUNK, WIDTH), F32),
            jax.ShapeDtypeStruct((2,), F32),
        ),
        in_specs=[smem, vmem, vmem],
        out_specs=(vmem, vmem, smem),
        scratch_shapes=[
            pltpu.VMEM((2048, WIDTH), BF16),
            pltpu.VMEM((1024, WIDTH), BF16),
            pltpu.VMEM((2048, 1024), F32),
            pltpu.VMEM((2048, 1024), BF16),
            pltpu.VMEM((2048, 128), F32),
            pltpu.VMEM((2048, 128), F32),
            pltpu.VMEM((8, 1024), F32),
            pltpu.VMEM((8, 1024), F32),
            pltpu.VMEM((16, 128), F32),
            pltpu.VMEM((15, 16, 128), F32),
            pltpu.VMEM((8, 128), F32),
            pltpu.VMEM((7, 8, 128), F32),
            pltpu.VMEM((16, 128), F32),
            pltpu.VMEM((8, 128), F32),
            pltpu.VMEM((1, 1024), F32),
            pltpu.VMEM((1024, WIDTH), F32),
            pltpu.VMEM((1024, WIDTH), F32),
            pltpu.VMEM((1024, WIDTH), BF16),
            pltpu.VMEM((1024, WIDTH), BF16),
            pltpu.VMEM((2, 1024, WIDTH), BF16),
            pltpu.VMEM((2, 7 * CHUNK, WIDTH), BF16),
            pltpu.VMEM((16, 128), F32),
            pltpu.VMEM((15, 16, 128), F32),
            pltpu.VMEM((16, 128), F32),
            pltpu.VMEM((7, 16, 128), F32),
            dma((2, 21)),
            dma((2, 21)),
            dma((32,)),
            dma((32,)),
            dma((15,)),
            dma((15,)),
            dma((7,)),
            dma((7,)),
            dma((2, 21)),
            dma((2, 21)),
            dma((22,)),
            dma((22,)),
        ],
        compiler_params=pltpu.CompilerParams(
            collective_id=0, has_side_effects=True, vmem_limit_bytes=60 * 2**20
        ),
        name="contrastive",
    )(logit_scale, image_features, text_features)
    return sums[0:1], image_grad, text_grad, sums[1:2]


def solution(mesh):
    in_specs = (P(("row", "col"), None), P(("col", "row"), None), P())
    out_specs = (P(), P(("row", "col"), None), P(("col", "row"), None), P())
    return jax.shard_map(local, mesh=mesh, in_specs=in_specs, out_specs=out_specs, check_vma=False)
```

time: 639 us -> 75.3 us (0.12)
  blocking collectives: 329 us -> 0 us
  waiting for transfers between devices: 143 us -> 0 us
  matrix products: 78.6 us -> 0 us
  Pallas kernels: 0 us -> 69.9 us
  other arithmetic: 34.7 us -> 0 us
  loops' own time: 21.6 us -> 0 us
  between operations: 19.4 us -> 1.3 us
  local copies, waits for them, and re-layouts: 10.5 us -> 3.89 us
    psum x3 -> x0, blocking collectives: 198 us -> none  [the longest x1 124 us: local(): row_total = lax.psum(row_total * jnp.exp(row_peak - row_top), 'col')]
    pmax x2 -> x0, blocking collectives: 131 us -> none  [the longest x1 122 us: local(): row_top = lax.pmax(row_peak, 'col')]
    all_gather x2 -> x0, waiting for transfers between devices: 80.1 us -> none  [the longest x1 57.4 us: local(): lax.all_gather(image_hat.astype(jnp.bfloat16), 'col', axis=0, tiled=True)]
    dot_general x25 -> x0, matrix products: 78.6 us -> none  [the longest x16 45.4 us: contract_rows(): lax.dot_general(left, right, (((1,), (1,)), ((), ())), preferred_element_...]
    pallas_call x0 -> x1, Pallas kernels: none -> 69.9 us  [local(): pl.pallas_call(kernel, out_shape=(jax.ShapeDtypeStruct((CHUNK, WIDTH), F3...]
    reduce_scatter x2 -> x0, waiting for transfers between devices: 62.5 us -> none  [the longest x1 62.5 us: local(): lax.psum_scatter(scale * jnp.dot(grad_tile, text_cols, preferred_element_...]
    another operation x2 -> x0, loops' own time: 21.6 us -> none  [the longest x1 10.9 us: local(): lax.scan(forward, init, (image_blocks, starts))]
    reduce_sum x14 -> x0, other arithmetic: 14.9 us -> none  [the longest x8 8.73 us: forward(): row_total = jnp.sum(jnp.exp(values - row_peak[:, None]), axis=1)]
  transfers between devices with their start and end apart: 4 -> 0, of which waited for: 3 -> 0; matrix products, arithmetic and copies ran while one was open for 3% -> 0% of each run, Pallas kernels for 0% -> 0%
where the time goes in v1:
time: 75.3 us; the launch traced here: 75.1 us
  Pallas kernels  69.9 us (93%)
  local copies, waits for them, and re-layouts  3.89 us (5%)
  between operations  1.3 us (2%)
    pallas_call x1, Pallas kernels, local(): pl.pallas_call(kernel, out_shape=(jax.ShapeDtypeStruct((CHUNK, WIDTH), F3...  69.9 us
    unnamed x6, local copies, waits for them, and re-layouts  3.31 us

profile of v1, /device:TPU:1, one launch (start us, length us, event | category | flops | bytes accessed | tf_op | source)
XLA Modules:
  0.0 75.1 jit_solution(17872738964376096151)
XLA Ops:
  1.3 69.9 %contrastive.1 = (f32[128,1024]{1,0:T(8,128)}, f32[128,1024]{1,0:T(8,128)}, f32[2]{0:T(128)}) custom-call(f32[1]{0:T(128)S(6)} %copy.9.scale_ref, f32[128,1024]{1,0:T(8,128)} %image_ref.1, f32[128,1024]{1,0:T(8,128)} %text_ref.1), custom_call_target="tpu_custom_call" | custom-call | tf_op jit(solution)/shard_map/contrastive/pallas_call | solution.py:434
  71.2 0.0 copy-start.1
  71.2 0.6 copy-done.1
  71.8 0.6 fusion
  72.3 0.0 copy-start
  72.3 1.9 %copy.10 = f32[128,1024]{1,0:T(8,128)} copy(f32[128,1024]{1,0:T(8,128)} %get-tuple-element.17) | data formatting | bytes 1048576
  74.3 0.0 copy-done
  74.3 0.8 %copy.11 = f32[128,1024]{1,0:T(8,128)} copy(f32[128,1024]{1,0:T(8,128)S(1)} %copy-done) | data formatting | bytes 1048576
Async XLA Ops:
  71.2 0.6 copy-start.1
  72.3 1.9 %copy-start = (f32[128,1024]{1,0:T(8,128)S(1)}, f32[128,1024]{1,0:T(8,128)}, u32[]{:S(2)}) copy-start(f32[128,1024]{1,0:T(8,128)} %get-tuple-element.18) | copy-start | bytes 1572868

commit v2 on v1

v2 whole, which is shorter than its diff:
```python
import functools

import jax
import jax.numpy as jnp
from jax import lax
from jax.experimental import pallas as pl
from jax.experimental.pallas import tpu as pltpu
from jax.sharding import PartitionSpec as P

MESH = pl.DeviceIdType.MESH
EPS = 1e-06
LOG2E = 1.4426950408889634
LN2 = 0.6931471805599453
SHIFT = 34.0
TINY = 2.0**-60

CHUNK = 128
WIDTH = 1024
ORDER = (0, 1, 2, 4, 5, 3, 6, 7)
RANK = tuple(ORDER.index(q) for q in range(8))
PARTS = ((0, 48, 0, 896, 0), (48, 48, 0, 896, 1), (96, 32, 0, 1024, 2), (0, 96, 896, 128, 2))
N_PARTS = len(PARTS)
BF16 = jnp.bfloat16
F32 = jnp.float32


def stage_dim(part, stage):
    return (PARTS[part][4] + stage) % 3


def last_stage(q, part):
    stage = -1
    for t in range(3):
        if q >> stage_dim(part, t) & 1:
            stage = t
    return stage


def log2(x):
    return jnp.log(x) * LOG2E


def nt(a, b):
    return lax.dot_general(a, b, (((1,), (1,)), ((), ())), preferred_element_type=F32)


def nn(a, b):
    return lax.dot_general(a, b, (((1,), (0,)), ((), ())), preferred_element_type=F32)


def tn(a, b):
    return lax.dot_general(a, b, (((0,), (0,)), ((), ())), preferred_element_type=F32)


def flip_image(c):
    return c + 1 - 2 * lax.rem(c, 2)


def flip_text(c):
    return 3 - c


def kernel(
    scale_ref, image_ref, text_ref,
    image_out, text_out, sums_out,
    scale_s, feat_s, lse_s, eye_s,
    img, txt, u_s, grad_s, hi_s, lo_s, colhi_s, collo_s,
    rowl_s, rowl_r, coll_s, coll_r, rlse_s, clse_s, crow_s,
    a_img, a_txt, core_s, core_r, rs_s, rs_r,
    part_s, part_r, part2_s, part2_r,
    load_sem, ag_send, ag_recv, core_send, core_recv,
    lse_send, lse_recv, csum_send, csum_recv, rs_send, rs_recv, tot_send, tot_recv,
):
    z = lax.axis_index("row")
    c = lax.axis_index("col")
    x, y, k = c // 8, lax.rem(c // 2, 4), lax.rem(c, 2)
    at = (x, y, z)
    flipped = (tuple(flip_image(v) for v in at), tuple(flip_text(v) for v in at))

    def place(side, q, other_core=0):
        px, py, pz = (flipped[side][d] if q >> d & 1 else at[d] for d in range(3))
        return {"row": pz, "col": (px * 4 + py) * 2 + (1 - k if other_core else k)}

    def remote(src, dst, send, recv, device):
        return pltpu.make_async_remote_copy(
            src_ref=src, dst_ref=dst, send_sem=send, recv_sem=recv, device_id=device, device_id_type=MESH
        )

    loads = [
        pltpu.make_async_copy(image_ref, feat_s.at[0], load_sem.at[0]),
        pltpu.make_async_copy(text_ref, feat_s.at[1], load_sem.at[1]),
        pltpu.make_async_copy(scale_ref, scale_s, load_sem.at[2]),
    ]
    for load in loads:
        load.start()
    peers = [place(0, 0, 1)] + [place(side, 1 << d) for side in range(2) for d in range(3)]
    barrier = pltpu.get_barrier_semaphore()
    for peer in peers:
        pl.semaphore_signal(barrier, inc=1, device_id=peer, device_id_type=MESH)

    def normalized(side):
        v = feat_s[side]
        return v * lax.rsqrt(jnp.sum(v * v, axis=1, keepdims=True) + EPS)

    loads[0].wait()
    img[pl.ds(0, CHUNK), :] = normalized(0).astype(BF16)
    loads[1].wait()
    txt[pl.ds(0, CHUNK), :] = normalized(1).astype(BF16)
    loads[2].wait()
    scale = jnp.exp(jnp.full((8, 128), scale_s[0], F32))[0:1, 0:1]
    unit = scale * LOG2E
    hi_s[...] = jnp.zeros_like(hi_s)
    lo_s[...] = jnp.zeros_like(lo_s)
    colhi_s[...] = jnp.zeros_like(colhi_s)
    collo_s[...] = jnp.zeros_like(collo_s)

    eye = lax.broadcasted_iota(jnp.int32, (CHUNK, CHUNK), 0) == lax.broadcasted_iota(jnp.int32, (CHUNK, CHUNK), 1)
    eye_s[pl.ds(0, CHUNK), :] = jnp.zeros((CHUNK, CHUNK), F32)
    eye_s[pl.ds(CHUNK, CHUNK), :] = jnp.where(eye, 1.0, 0.0)
    pl.semaphore_wait(barrier, len(peers))

    def area(part, base):
        row, rows, col, cols, _ = PARTS[part]
        return pl.ds(base + row, rows), pl.ds(col, cols)

    def gather_rows(side, q, part):
        return (img, txt)[side].at[area(part, RANK[q] * (2 * CHUNK if side == 0 else CHUNK))]

    def gather_copy(side, q, part):
        d = stage_dim(part, last_stage(q, part))
        i = (q - 1) * N_PARTS + part
        return remote(
            gather_rows(side, q ^ (1 << d), part), gather_rows(side, q, part),
            ag_send.at[side, i], ag_recv.at[side, i], place(side, 1 << d),
        )

    def core_copy(q, part):
        base = RANK[q] * 2 * CHUNK
        i = q * N_PARTS + part
        return remote(
            img.at[area(part, base)], img.at[area(part, base + CHUNK)],
            core_send.at[i], core_recv.at[i], place(0, 0, 1),
        )

    def arrive(q, first, *dims):
        for part in range(N_PARTS):
            if PARTS[part][4] == first:
                for side in range(2):
                    gather_copy(side, q, part).wait_recv()
                    for d in dims:
                        gather_copy(side, q | 1 << d, part).start()
                core_copy(q, part).start()

    def send_on(q, first):
        for part in range(N_PARTS):
            if PARTS[part][4] == first:
                for side in range(2):
                    gather_copy(side, q, part).start()

    def both_cores(*slots):
        for q in slots:
            for part in range(N_PARTS):
                core_copy(q, part).wait_recv()

    for t in range(3):
        for d in range(3):
            send_on(1 << d, (d - t) % 3)
    for part in range(N_PARTS):
        core_copy(0, part).start()

    def scores(row0, rows, col0, cols):
        for r in range(row0, row0 + rows, 256):
            u = nt(img[pl.ds(r, 256), :], txt[pl.ds(col0, cols), :]) * unit
            u_s[pl.ds(r, 256), pl.ds(col0, cols)] = u
            hi = jnp.exp2(u - SHIFT)
            lo = jnp.exp2(jnp.minimum(u, 0.0) + SHIFT)
            for e, row_s, col_s in ((hi, hi_s, colhi_s), (lo, lo_s, collo_s)):
                row = e[:, 0:128]
                for j in range(1, cols // 128):
                    row = row + e[:, j * 128 : (j + 1) * 128]
                row_s[pl.ds(r, 256), :] += row
                col_s[:, pl.ds(col0, cols)] += jnp.sum(e.reshape(32, 8, cols), axis=0)

    def joined(hi, lo):
        return jnp.where(hi > TINY, log2(hi) + SHIFT, log2(lo) - SHIFT)

    def absolute(side, q):
        bits = [lax.rem(v, 2) for v in at] if side == 0 else [v // 2 for v in at]
        bits = [1 - b if q >> d & 1 else b for d, b in enumerate(bits)]
        return bits[0] + 2 * bits[1] + 4 * bits[2]

    def row_index(q, other):
        return absolute(0, q) * 2 + (1 - k if other else k)

    def row_sums(q):
        for other in range(2):
            r = RANK[q] * 256 + other * CHUNK
            hi = jnp.sum(hi_s[pl.ds(r, CHUNK), :].T, axis=0, keepdims=True)
            lo = jnp.sum(lo_s[pl.ds(r, CHUNK), :].T, axis=0, keepdims=True)
            rowl_s[pl.ds(row_index(q, other), 1), :] = joined(hi, lo)

    arrive(1, 0, 1, 2)
    arrive(4, 2, 0)
    arrive(2, 1, 2)
    arrive(1, 2, 1)
    arrive(2, 0, 2)
    arrive(4, 1, 0)
    send_on(3, 1)
    send_on(6, 2)
    arrive(1, 1)
    arrive(2, 2)
    arrive(4, 0)
    both_cores(0, 1, 2, 4)
    scores(0, 1024, 0, 512)
    arrive(5, 2, 1)
    arrive(3, 0, 2)
    arrive(5, 0)
    arrive(6, 1, 0)
    arrive(5, 1)
    both_cores(5)
    scores(1024, 256, 0, 512)
    scores(0, 1280, 512, 128)
    arrive(3, 2)
    arrive(3, 1)
    arrive(6, 2)
    arrive(6, 0)
    both_cores(3, 6)
    scores(1280, 512, 0, 512)
    scores(1280, 512, 512, 128)
    scores(0, 1792, 640, 256)
    for part in range(3):
        arrive(7, part)
    scores(0, 1792, 896, 128)
    for q in ORDER[:7]:
        row_sums(q)
    both_cores(7)
    scores(1792, 256, 0, 512)
    scores(1792, 256, 512, 512)

    row_sums(7)
    colsum = joined(
        jnp.sum(colhi_s[...], axis=0, keepdims=True), jnp.sum(collo_s[...], axis=0, keepdims=True)
    )
    for q in range(8):
        coll_s[pl.ds(absolute(1, q), 1), :] = colsum[:, RANK[q] * 128 : (RANK[q] + 1) * 128]

    part_s[...] = jnp.zeros_like(part_s)

    def matching(q, other):
        ix, iy, iz = (flipped[0][d] if q >> d & 1 else at[d] for d in range(3))
        ik = 1 - k if other else k
        tx, ty, tk, tz = iz, ix, iy // 2, lax.rem(iy, 2) * 2 + ik
        here = tk == k
        slot = 0
        for d, t in enumerate((tx, ty, tz)):
            across = t == flipped[1][d]
            here = here & (across | (t == at[d]))
            slot = slot + jnp.where(across, 1 << d, 0)
        rank = sum(jnp.where(slot == q, RANK[q], 0) for q in range(1, 8))
        return jnp.where(here, rank, -1)

    matches = [matching(q, other) for q in ORDER for other in range(2)]

    def row_copy(j):
        return remote(rowl_s, rowl_r.at[j - 1], lse_send.at[j - 1], lse_recv.at[j - 1], place(0, j >> 1, j & 1))

    def col_copy(q):
        return remote(coll_s, coll_r.at[q - 1], csum_send.at[q - 1], csum_recv.at[q - 1], place(1, q))

    for q in range(1, 8):
        col_copy(q).start()
    for j in range(1, 16):
        row_copy(j).start()
    for i, rank in enumerate(matches):

        @pl.when(rank >= 0)
        def _():
            u = u_s[pl.ds(i * CHUNK, CHUNK), pl.ds(pl.multiple_of(rank * 128, 128), 128)]
            own = u * eye_s[pl.ds(CHUNK, CHUNK), :]
            part_s[pl.ds(0, 8), :] += -2.0 * jnp.sum(own.reshape(16, 8, 128), axis=0)

    for q in range(1, 8):
        col_copy(q).wait_recv()
    for j in range(1, 16):
        row_copy(j).wait_recv()

    def over(values):
        top = functools.reduce(jnp.maximum, values)
        return top + log2(functools.reduce(jnp.add, [jnp.exp2(v - top) for v in values]))

    rlse_s[...] = over([rowl_s[...]] + [rowl_r[j] for j in range(15)])
    clse_s[...] = over([coll_s[...]] + [coll_r[j] for j in range(7)])
    for q in range(8):
        crow_s[:, pl.ds(RANK[q] * 128, 128)] = clse_s[pl.ds(absolute(1, q), 1), :] + 1.0

    def spread(rank):
        for other in range(2):
            lse = rlse_s[pl.ds(row_index(ORDER[rank], other), 1), :] + 1.0
            lse_s[pl.ds(rank * 256 + other * CHUNK, CHUNK), :] = jnp.broadcast_to(lse, (CHUNK, CHUNK)).T

    def grads(blocks):
        total = jnp.zeros((8, 128), F32)
        for i, j in blocks:
            for other in range(2):
                here = pl.ds(i * 256 + other * CHUNK, CHUNK)
                at_col = pl.ds(j * 128, 128)
                u = u_s[here, at_col]
                flag = jnp.where(matches[i * 2 + other] == j, CHUNK, 0)
                own = eye_s[pl.ds(pl.multiple_of(flag, CHUNK), CHUNK), :]
                g = jnp.exp2(u - lse_s[here, :]) + jnp.exp2(u - crow_s[:, at_col]) - own
                grad_s[here, at_col] = g.astype(BF16)
                total = total + jnp.sum((g * u).reshape(16, 8, 128), axis=0)
        part_s[pl.ds(8, 8), :] += total

    part_s[pl.ds(0, 1), :] += rlse_s[pl.ds(row_index(0, 0), 1), :] + clse_s[pl.ds(absolute(1, 0), 1), :]

    def total_copy(stage, j):
        if stage == 0:
            src, dst, device = part_s, part_r, place(0, j >> 1, j & 1)
        else:
            src, dst, device = part2_s, part2_r, place(1, j)
        i = j - 1 + 15 * stage
        return remote(src, dst.at[j - 1], tot_send.at[i], tot_recv.at[i], device)

    def row_blocks(rank):
        return [(rank, j) for j in range(rank + 1)]

    def col_blocks(rank):
        return [(i, rank) for i in range(rank)]

    def image_product(q):
        r = RANK[q] * 256
        for n in range(0, WIDTH, 256):
            acc = nn(grad_s[pl.ds(r, 256), :], txt[:, pl.ds(n, 256)])
            a_img[pl.ds(RANK[q] * CHUNK, CHUNK), pl.ds(n, 256)] = acc[0:CHUNK]
            core_s[pl.ds(q * CHUNK, CHUNK), pl.ds(n, 256)] = acc[CHUNK:].astype(BF16)

    def sibling(q):
        here = pl.ds(q * CHUNK, CHUNK)
        return remote(core_s.at[here], core_r.at[here], core_send.at[8 * N_PARTS + q], core_recv.at[8 * N_PARTS + q], place(0, 0, 1))

    def join_cores(q):
        sibling(q).wait_recv()
        here = pl.ds(RANK[q] * CHUNK, CHUNK)
        a_img[here, :] += core_r[pl.ds(q * CHUNK, CHUNK), :].astype(F32)

    def text_product(q):
        here = pl.ds(RANK[q] * CHUNK, CHUNK)
        for n in range(0, WIDTH, 256):
            a_txt[here, pl.ds(n, 256)] = tn(grad_s[:, here], img[:, pl.ds(n, 256)])

    def region(q, part, stage):
        kept = [p for p in range(8) if all(not p >> stage_dim(part, t) & 1 for t in range(stage, 3))]
        return {2: 0, 1: 4, 0: 6}[stage] + kept.index(q)

    def sum_copy(side, q, part):
        stage = last_stage(q, part)
        d = stage_dim(part, stage)
        to = region(q ^ (1 << d), part, stage)
        i = to * N_PARTS + part
        return remote(
            rs_s.at[(side, *area(part, q * CHUNK))], rs_r.at[(side, *area(part, to * CHUNK))],
            rs_send.at[side, i], rs_recv.at[side, i], place(side, 1 << d),
        )

    def summed(side, q, part):
        acc = (a_img, a_txt)[side][area(part, RANK[q] * CHUNK)]
        for stage in range(2, last_stage(q, part), -1):
            d = stage_dim(part, stage)
            sum_copy(side, q | 1 << d, part).wait_recv()
            acc = acc + rs_r[(side, *area(part, region(q, part, stage) * CHUNK))].astype(F32)
        return acc

    def hand_on(side, q, part):
        rs_s[(side, *area(part, q * CHUNK))] = summed(side, q, part).astype(BF16)
        sum_copy(side, q, part).start()

    def rounds(side, slots, age):
        for q in slots:
            for part in range(N_PARTS):
                if 2 - last_stage(q, part) == age:
                    hand_on(side, q, part)

    def image_step(q):
        image_product(q)
        sibling(q).start()

    def text_step(q):
        if q:
            grads(row_blocks(RANK[q] - 1) + col_blocks(RANK[q] - 1))
        text_product(q)
        rounds(1, (q,), 0)

    def join(q):
        join_cores(q)
        rounds(0, (q,), 0)

    spread(7)
    grads(row_blocks(7))
    image_step(7)
    for rank in range(6, -1, -1):
        spread(rank)
    grads(col_blocks(7))
    text_step(7)
    image_step(6)
    join(7)
    text_step(6)
    image_step(3)
    join(6)
    text_step(3)
    image_step(5)
    join(3)
    text_step(5)
    rounds(1, (6, 3, 5), 1)
    image_step(4)
    join(5)
    rounds(0, (6, 3, 5), 1)
    text_step(4)
    image_step(2)
    join(4)
    text_step(2)
    image_step(1)
    join(2)
    text_step(1)
    for j in range(1, 16):
        total_copy(0, j).start()
    rounds(1, (4, 2, 1), 1)
    image_step(0)
    join(1)
    rounds(0, (4, 2, 1), 1)
    text_step(0)
    rounds(1, (4, 2, 1), 2)
    rounds(0, (4, 2, 1), 2)
    for j in range(1, 16):
        total_copy(0, j).wait_recv()
    part2_s[...] = functools.reduce(jnp.add, [part_s[...]] + [part_r[j] for j in range(15)])
    for q in range(1, 8):
        total_copy(1, q).start()
    join_cores(0)

    for side, out in ((1, text_out), (0, image_out)):
        for part in range(N_PARTS):
            out[area(part, 0)] = summed(side, 0, part)
        for row in range(0, CHUNK, 32):
            here = pl.ds(row, 32)
            v = feat_s[side, here, :]
            inverse = lax.rsqrt(jnp.sum(v * v, axis=1, keepdims=True) + EPS)
            hat = v * inverse
            g = out[here, :] * scale
            out[here, :] = inverse * (g - hat * jnp.sum(hat * g, axis=1, keepdims=True))

    for q in range(1, 8):
        total_copy(1, q).wait_recv()
    totals = functools.reduce(jnp.add, [part2_s[...]] + [part2_r[j] for j in range(7)])
    pairs = 128.0 * CHUNK
    sums_out[0] = jnp.sum(totals[0:8]) * (LN2 / (2.0 * pairs))
    sums_out[1] = jnp.sum(totals[8:16]) * (LN2 / pairs)

    for side in range(2):
        for q in range(1, 8):
            for part in range(N_PARTS):
                gather_copy(side, q, part).wait_send()
                sum_copy(side, q, part).wait_send()
    for q in range(8):
        sibling(q).wait_send()
        for part in range(N_PARTS):
            core_copy(q, part).wait_send()
    for j in range(1, 16):
        row_copy(j).wait_send()
        total_copy(0, j).wait_send()
    for q in range(1, 8):
        col_copy(q).wait_send()
        total_copy(1, q).wait_send()


def deliver(image_ref, text_ref, sums_ref, loss_out, image_out, text_out, scale_out, sem):
    copies = [
        pltpu.make_async_copy(image_ref, image_out, sem.at[0]),
        pltpu.make_async_copy(text_ref, text_out, sem.at[1]),
    ]
    for copy in copies:
        copy.start()
    loss_out[0] = sums_ref[0]
    scale_out[0] = sums_ref[1]
    for copy in copies:
        copy.wait()


def local(image_features, text_features, logit_scale):
    hbm = pl.BlockSpec(memory_space=pltpu.HBM)
    vmem = pl.BlockSpec(memory_space=pltpu.VMEM)
    smem = pl.BlockSpec(memory_space=pltpu.SMEM)
    dma = pltpu.SemaphoreType.DMA
    image_grad, text_grad, sums = pl.pallas_call(
        kernel,
        out_shape=(
            pltpu.VMEM((CHUNK, WIDTH), F32),
            pltpu.VMEM((CHUNK, WIDTH), F32),
            pltpu.SMEM((2,), F32),
        ),
        in_specs=[hbm] * 3,
        out_specs=(vmem, vmem, smem),
        scratch_shapes=[
            pltpu.SMEM((1,), F32),
            pltpu.VMEM((2, CHUNK, WIDTH), F32),
            pltpu.VMEM((2048, 128), F32),
            pltpu.VMEM((2 * CHUNK, CHUNK), F32),
            pltpu.VMEM((2048, WIDTH), BF16),
            pltpu.VMEM((1024, WIDTH), BF16),
            pltpu.VMEM((2048, 1024), F32),
            pltpu.VMEM((2048, 1024), BF16),
            pltpu.VMEM((2048, 128), F32),
            pltpu.VMEM((2048, 128), F32),
            pltpu.VMEM((8, 1024), F32),
            pltpu.VMEM((8, 1024), F32),
            pltpu.VMEM((16, 128), F32),
            pltpu.VMEM((15, 16, 128), F32),
            pltpu.VMEM((8, 128), F32),
            pltpu.VMEM((7, 8, 128), F32),
            pltpu.VMEM((16, 128), F32),
            pltpu.VMEM((8, 128), F32),
            pltpu.VMEM((1, 1024), F32),
            pltpu.VMEM((1024, WIDTH), F32),
            pltpu.VMEM((1024, WIDTH), F32),
            pltpu.VMEM((1024, WIDTH), BF16),
            pltpu.VMEM((1024, WIDTH), BF16),
            pltpu.VMEM((2, 1024, WIDTH), BF16),
            pltpu.VMEM((2, 7 * CHUNK, WIDTH), BF16),
            pltpu.VMEM((16, 128), F32),
            pltpu.VMEM((15, 16, 128), F32),
            pltpu.VMEM((16, 128), F32),
            pltpu.VMEM((7, 16, 128), F32),
            dma((3,)),
            dma((2, 7 * N_PARTS)),
            dma((2, 7 * N_PARTS)),
            dma((8 * N_PARTS + 8,)),
            dma((8 * N_PARTS + 8,)),
            dma((15,)),
            dma((15,)),
            dma((7,)),
            dma((7,)),
            dma((2, 7 * N_PARTS)),
            dma((2, 7 * N_PARTS)),
            dma((22,)),
            dma((22,)),
        ],
        compiler_params=pltpu.CompilerParams(
            collective_id=0, has_side_effects=True, vmem_limit_bytes=60 * 2**20
        ),
        name="contrastive",
    )(logit_scale, image_features, text_features)
    one = jax.ShapeDtypeStruct((1,), F32)
    grad = jax.ShapeDtypeStruct((CHUNK, WIDTH), F32)
    return pl.pallas_call(
        deliver,
        out_shape=(one, grad, grad, one),
        in_specs=[vmem, vmem, smem],
        out_specs=(smem, hbm, hbm, smem),
        scratch_shapes=[dma((2,))],
        name="finish",
    )(image_grad, text_grad, sums)


def solution(mesh):
    in_specs = (P(("row", "col"), None), P(("col", "row"), None), P())
    out_specs = (P(), P(("row", "col"), None), P(("col", "row"), None), P())
    return jax.shard_map(local, mesh=mesh, in_specs=in_specs, out_specs=out_specs, check_vma=False)
```

time: 75.3 us -> 67.9 us (0.902)
  Pallas kernels: 69.9 us -> 64.7 us
  local copies, waits for them, and re-layouts: 3.89 us -> 1.58 us
    pallas_call x1 -> x2, Pallas kernels: 69.9 us -> 64.7 us  [the longest x1 62 us: local(): pl.pallas_call(kernel, out_shape=(pltpu.VMEM((CHUNK, WIDTH), F32), pltpu....]
    unnamed x6 -> x4, local copies, waits for them, and re-layouts: 3.31 us -> 1.58 us
where the time goes in v2:
time: 67.9 us; the launch traced here: 67.7 us
  Pallas kernels  64.7 us (95%)
  local copies, waits for them, and re-layouts  1.58 us (2%)
  between operations  1.48 us (2%)
    pallas_call x1, Pallas kernels, local(): pl.pallas_call(kernel, out_shape=(pltpu.VMEM((CHUNK, WIDTH), F32), pltpu....  62 us
    pallas_call x1, Pallas kernels, local(): pl.pallas_call(deliver, out_shape=(one, grad, grad, one), in_specs=[vmem,...  2.71 us
    unnamed x4, local copies, waits for them, and re-layouts  1.58 us

profile of v2, /device:TPU:1, one launch (start us, length us, event | category | flops | bytes accessed | tf_op | source)
XLA Modules:
  0.0 67.7 jit_solution(6540622337732734614)
XLA Ops:
  1.3 62.0 %contrastive.1 = (f32[128,1024]{1,0:T(8,128)S(1)}, f32[128,1024]{1,0:T(8,128)S(1)}, f32[2]{0:T(128)S(4)}) custom-call(f32[1]{0:T(128)S(6)} %copy.7.scale_ref, f32[128,1024]{1,0:T(8,128)} %image_ref.1, f32[128,1024]{1,0:T(8,128)} %text_ref.1), custom_call_target="tpu_custom_call" | custom-call | tf_op jit(solution)/shard_map/contrastive/pallas_call | solution.py:494
  63.2 0.0 copy-start
  63.3 0.8 %copy-done = f32[128,1024]{1,0:T(8,128)} copy-done((f32[128,1024]{1,0:T(8,128)}, f32[128,1024]{1,0:T(8,128)S(1)}, u32[]{:S(2)}) %copy-start) | copy-done | bytes 524312
  64.0 0.0 copy-start.1
  64.0 0.8 %copy-done.1 = f32[128,1024]{1,0:T(8,128)} copy-done((f32[128,1024]{1,0:T(8,128)}, f32[128,1024]{1,0:T(8,128)S(1)}, u32[]{:S(2)}) %copy-start.1) | copy-done | bytes 524312
  64.8 2.7 %finish.1 = (f32[1]{0:T(128)}, f32[128,1024]{1,0:T(8,128)}, f32[128,1024]{1,0:T(8,128)}, f32[1]{0:T(128)}) custom-call(f32[128,1024]{1,0:T(8,128)} %copy-done, f32[128,1024]{1,0:T(8,128)} %copy-done.1, f32[2]{0:T(128)S(4)} %get-tuple-element.9.sums_ref), custom_call_target="tpu_custom_call" | custom-call | tf_op jit(solution)/shard_map/finish/pallas_call | solution.py:554
Async XLA Ops:
  63.2 0.8 %copy-start = (f32[128,1024]{1,0:T(8,128)}, f32[128,1024]{1,0:T(8,128)S(1)}, u32[]{:S(2)}) copy-start(f32[128,1024]{1,0:T(8,128)S(1)} %get-tuple-element.7.image_ref) | copy-start | bytes 1572868
  64.0 0.8 %copy-start.1 = (f32[128,1024]{1,0:T(8,128)}, f32[128,1024]{1,0:T(8,128)S(1)}, u32[]{:S(2)}) copy-start(f32[128,1024]{1,0:T(8,128)S(1)} %get-tuple-element.8.text_ref) | copy-start | bytes 1572868

commit v3 on v2

--- a/solution.py
+++ b/solution.py
@@ -19,7 +19,7 @@
 ORDER = (0, 1, 2, 4, 5, 3, 6, 7)
 RANK = tuple(ORDER.index(q) for q in range(8))
 PARTS = ((0, 48, 0, 896, 0), (48, 48, 0, 896, 1), (96, 32, 0, 1024, 2), (0, 96, 896, 128, 2))
-N_PARTS = len(PARTS)
+N_PARTS = 4
 BF16 = jnp.bfloat16
 F32 = jnp.float32
 
@@ -62,12 +62,12 @@
 
 def kernel(
     scale_ref, image_ref, text_ref,
-    image_out, text_out, sums_out,
+    loss_out, image_out, text_out, scale_out,
     scale_s, feat_s, lse_s, eye_s,
-    img, txt, u_s, grad_s, hi_s, lo_s, colhi_s, collo_s,
+    img, txt, u_s, grad_s, flip_s, row_acc, col_acc, rowm_s, colm_s,
     rowl_s, rowl_r, coll_s, coll_r, rlse_s, clse_s, crow_s,
     a_img, a_txt, core_s, core_r, rs_s, rs_r,
-    part_s, part_r, part2_s, part2_r,
+    part_s, part_r, part2_s, part2_r, part3_s, part3_r,
     load_sem, ag_send, ag_recv, core_send, core_recv,
     lse_send, lse_recv, csum_send, csum_recv, rs_send, rs_recv, tot_send, tot_recv,
 ):
@@ -93,6 +93,9 @@
     ]
     for load in loads:
         load.start()
+    def taken(ref, sem):
+        pltpu.make_async_copy(ref, ref, sem).wait()
+
     peers = [place(0, 0, 1)] + [place(side, 1 << d) for side in range(2) for d in range(3)]
     barrier = pltpu.get_barrier_semaphore()
     for peer in peers:
@@ -109,10 +112,8 @@
     loads[2].wait()
     scale = jnp.exp(jnp.full((8, 128), scale_s[0], F32))[0:1, 0:1]
     unit = scale * LOG2E
-    hi_s[...] = jnp.zeros_like(hi_s)
-    lo_s[...] = jnp.zeros_like(lo_s)
-    colhi_s[...] = jnp.zeros_like(colhi_s)
-    collo_s[...] = jnp.zeros_like(collo_s)
+    row_acc[...] = jnp.zeros_like(row_acc)
+    col_acc[...] = jnp.zeros_like(col_acc)
 
     eye = lax.broadcasted_iota(jnp.int32, (CHUNK, CHUNK), 0) == lax.broadcasted_iota(jnp.int32, (CHUNK, CHUNK), 1)
     eye_s[pl.ds(0, CHUNK), :] = jnp.zeros((CHUNK, CHUNK), F32)
@@ -131,15 +132,14 @@
         i = (q - 1) * N_PARTS + part
         return remote(
             gather_rows(side, q ^ (1 << d), part), gather_rows(side, q, part),
-            ag_send.at[side, i], ag_recv.at[side, i], place(side, 1 << d),
+            ag_send.at[side], ag_recv.at[side, i], place(side, 1 << d),
         )
 
     def core_copy(q, part):
         base = RANK[q] * 2 * CHUNK
-        i = q * N_PARTS + part
         return remote(
             img.at[area(part, base)], img.at[area(part, base + CHUNK)],
-            core_send.at[i], core_recv.at[i], place(0, 0, 1),
+            core_send.at[0], core_recv.at[q], place(0, 0, 1),
         )
 
     def arrive(q, first, *dims):
@@ -159,8 +159,8 @@
 
     def both_cores(*slots):
         for q in slots:
-            for part in range(N_PARTS):
-                core_copy(q, part).wait_recv()
+            taken(img.at[pl.ds(RANK[q] * 256 + CHUNK, CHUNK)], core_recv.at[q])
+
 
     for t in range(3):
         for d in range(3):
@@ -174,15 +174,18 @@
             u_s[pl.ds(r, 256), pl.ds(col0, cols)] = u
             hi = jnp.exp2(u - SHIFT)
             lo = jnp.exp2(jnp.minimum(u, 0.0) + SHIFT)
-            for e, row_s, col_s in ((hi, hi_s, colhi_s), (lo, lo_s, collo_s)):
+            for i, e in enumerate((hi, lo, hi * u, lo * u)):
                 row = e[:, 0:128]
                 for j in range(1, cols // 128):
                     row = row + e[:, j * 128 : (j + 1) * 128]
-                row_s[pl.ds(r, 256), :] += row
-                col_s[:, pl.ds(col0, cols)] += jnp.sum(e.reshape(32, 8, cols), axis=0)
+                row_acc[i, pl.ds(r, 256), :] += row
+                col_acc[i, :, pl.ds(col0, cols)] += jnp.sum(e.reshape(32, 8, cols), axis=0)
 
     def joined(hi, lo):
         return jnp.where(hi > TINY, log2(hi) + SHIFT, log2(lo) - SHIFT)
+
+    def averaged(hi, lo, weighted_hi, weighted_lo):
+        return jnp.where(hi > TINY, weighted_hi / hi, weighted_lo / lo)
 
     def absolute(side, q):
         bits = [lax.rem(v, 2) for v in at] if side == 0 else [v // 2 for v in at]
@@ -195,9 +198,10 @@
     def row_sums(q):
         for other in range(2):
             r = RANK[q] * 256 + other * CHUNK
-            hi = jnp.sum(hi_s[pl.ds(r, CHUNK), :].T, axis=0, keepdims=True)
-            lo = jnp.sum(lo_s[pl.ds(r, CHUNK), :].T, axis=0, keepdims=True)
-            rowl_s[pl.ds(row_index(q, other), 1), :] = joined(hi, lo)
+            sums = [jnp.sum(row_acc[i, pl.ds(r, CHUNK), :].T, axis=0, keepdims=True) for i in range(4)]
+            here = pl.ds(row_index(q, other), 1)
+            rowl_s[here, :] = joined(*sums[:2])
+            rowm_s[here, :] = averaged(*sums)
 
     arrive(1, 0, 1, 2)
     arrive(4, 2, 0)
@@ -230,6 +234,14 @@
     scores(0, 1792, 640, 256)
     for part in range(3):
         arrive(7, part)
+
+    def gathered():
+        taken(img.at[pl.ds(0, 7 * CHUNK)], ag_send.at[0])
+        taken(txt.at[pl.ds(0, 7 * CHUNK)], ag_send.at[1])
+        taken(img.at[pl.ds(0, 8 * CHUNK)], core_send.at[0])
+        taken(rowl_r, lse_send.at[0])
+        taken(coll_r, csum_send.at[0])
+
     scores(0, 1792, 896, 128)
     for q in ORDER[:7]:
         row_sums(q)
@@ -238,12 +250,12 @@
     scores(1792, 256, 512, 512)
 
     row_sums(7)
-    colsum = joined(
-        jnp.sum(colhi_s[...], axis=0, keepdims=True), jnp.sum(collo_s[...], axis=0, keepdims=True)
-    )
+    sums = [jnp.sum(col_acc[i], axis=0, keepdims=True) for i in range(4)]
+    col_lse, col_mean = joined(*sums[:2]), averaged(*sums)
     for q in range(8):
-        coll_s[pl.ds(absolute(1, q), 1), :] = colsum[:, RANK[q] * 128 : (RANK[q] + 1) * 128]
-
+        here, at_col = pl.ds(absolute(1, q), 1), slice(RANK[q] * 128, (RANK[q] + 1) * 128)
+        coll_s[here, :] = col_lse[:, at_col]
+        colm_s[here, :] = col_mean[:, at_col]
     part_s[...] = jnp.zeros_like(part_s)
 
     def matching(q, other):
@@ -262,10 +274,10 @@
     matches = [matching(q, other) for q in ORDER for other in range(2)]
 
     def row_copy(j):
-        return remote(rowl_s, rowl_r.at[j - 1], lse_send.at[j - 1], lse_recv.at[j - 1], place(0, j >> 1, j & 1))
+        return remote(rowl_s, rowl_r.at[j - 1], lse_send.at[0], lse_recv.at[0], place(0, j >> 1, j & 1))
 
     def col_copy(q):
-        return remote(coll_s, coll_r.at[q - 1], csum_send.at[q - 1], csum_recv.at[q - 1], place(1, q))
+        return remote(coll_s, coll_r.at[q - 1], csum_send.at[0], csum_recv.at[0], place(1, q))
 
     for q in range(1, 8):
         col_copy(q).start()
@@ -277,12 +289,12 @@
         def _():
             u = u_s[pl.ds(i * CHUNK, CHUNK), pl.ds(pl.multiple_of(rank * 128, 128), 128)]
             own = u * eye_s[pl.ds(CHUNK, CHUNK), :]
-            part_s[pl.ds(0, 8), :] += -2.0 * jnp.sum(own.reshape(16, 8, 128), axis=0)
-
-    for q in range(1, 8):
-        col_copy(q).wait_recv()
-    for j in range(1, 16):
-        row_copy(j).wait_recv()
+            own = jnp.sum(own.reshape(16, 8, 128), axis=0)
+            part_s[pl.ds(0, 8), :] += -2.0 * own
+            part_s[pl.ds(8, 8), :] += -own
+
+    taken(coll_r, csum_recv.at[0])
+    taken(rowl_r, lse_recv.at[0])
 
     def over(values):
         top = functools.reduce(jnp.maximum, values)
@@ -299,7 +311,6 @@
             lse_s[pl.ds(rank * 256 + other * CHUNK, CHUNK), :] = jnp.broadcast_to(lse, (CHUNK, CHUNK)).T
 
     def grads(blocks):
-        total = jnp.zeros((8, 128), F32)
         for i, j in blocks:
             for other in range(2):
                 here = pl.ds(i * 256 + other * CHUNK, CHUNK)
@@ -308,19 +319,20 @@
                 flag = jnp.where(matches[i * 2 + other] == j, CHUNK, 0)
                 own = eye_s[pl.ds(pl.multiple_of(flag, CHUNK), CHUNK), :]
                 g = jnp.exp2(u - lse_s[here, :]) + jnp.exp2(u - crow_s[:, at_col]) - own
-                grad_s[here, at_col] = g.astype(BF16)
-                total = total + jnp.sum((g * u).reshape(16, 8, 128), axis=0)
-        part_s[pl.ds(8, 8), :] += total
-
+                low = g.astype(BF16)
+                grad_s[here, at_col] = low
+                flip_s[at_col, here] = low.T
+
+    weighted = jnp.exp2(rowl_s[...] - rlse_s[...]) * rowm_s[...]
+    weighted = weighted[0:8] + weighted[8:16] + jnp.exp2(coll_s[...] - clse_s[...]) * colm_s[...]
+    part_s[pl.ds(8, 8), :] += 0.5 * weighted
     part_s[pl.ds(0, 1), :] += rlse_s[pl.ds(row_index(0, 0), 1), :] + clse_s[pl.ds(absolute(1, 0), 1), :]
 
-    def total_copy(stage, j):
+    def total_copy(stage, q):
         if stage == 0:
-            src, dst, device = part_s, part_r, place(0, j >> 1, j & 1)
-        else:
-            src, dst, device = part2_s, part2_r, place(1, j)
-        i = j - 1 + 15 * stage
-        return remote(src, dst.at[j - 1], tot_send.at[i], tot_recv.at[i], device)
+            return remote(part_s, part_r, tot_send.at[0], tot_recv.at[0], place(0, 0, 1))
+        src, dst = ((part2_s, part2_r), (part3_s, part3_r))[stage - 1]
+        return remote(src, dst.at[q - 1], tot_send.at[stage], tot_recv.at[stage], place(stage - 1, q))
 
     def row_blocks(rank):
         return [(rank, j) for j in range(rank + 1)]
@@ -337,17 +349,15 @@
 
     def sibling(q):
         here = pl.ds(q * CHUNK, CHUNK)
-        return remote(core_s.at[here], core_r.at[here], core_send.at[8 * N_PARTS + q], core_recv.at[8 * N_PARTS + q], place(0, 0, 1))
-
-    def join_cores(q):
-        sibling(q).wait_recv()
-        here = pl.ds(RANK[q] * CHUNK, CHUNK)
-        a_img[here, :] += core_r[pl.ds(q * CHUNK, CHUNK), :].astype(F32)
+        return remote(core_s.at[here], core_r.at[here], core_send.at[1], core_recv.at[8 + q], place(0, 0, 1))
 
     def text_product(q):
         here = pl.ds(RANK[q] * CHUNK, CHUNK)
         for n in range(0, WIDTH, 256):
-            a_txt[here, pl.ds(n, 256)] = tn(grad_s[:, here], img[:, pl.ds(n, 256)])
+            acc = nn(flip_s[here, :], img[:, pl.ds(n, 256)])
+            a_txt[here, pl.ds(n, 256)] = acc
+            if q:
+                rs_s[1, pl.ds(q * CHUNK, CHUNK), pl.ds(n, 256)] = acc.astype(BF16)
 
     def region(q, part, stage):
         kept = [p for p in range(8) if all(not p >> stage_dim(part, t) & 1 for t in range(stage, 3))]
@@ -360,11 +370,13 @@
         i = to * N_PARTS + part
         return remote(
             rs_s.at[(side, *area(part, q * CHUNK))], rs_r.at[(side, *area(part, to * CHUNK))],
-            rs_send.at[side, i], rs_recv.at[side, i], place(side, 1 << d),
+            rs_send.at[side], rs_recv.at[side, i], place(side, 1 << d),
         )
 
     def summed(side, q, part):
         acc = (a_img, a_txt)[side][area(part, RANK[q] * CHUNK)]
+        if side == 0:
+            acc = acc + core_r[area(part, q * CHUNK)].astype(F32)
         for stage in range(2, last_stage(q, part), -1):
             d = stage_dim(part, stage)
             sum_copy(side, q | 1 << d, part).wait_recv()
@@ -372,7 +384,8 @@
         return acc
 
     def hand_on(side, q, part):
-        rs_s[(side, *area(part, q * CHUNK))] = summed(side, q, part).astype(BF16)
+        if not (side == 1 and last_stage(q, part) == 2):
+            rs_s[(side, *area(part, q * CHUNK))] = summed(side, q, part).astype(BF16)
         sum_copy(side, q, part).start()
 
     def rounds(side, slots, age):
@@ -381,62 +394,53 @@
                 if 2 - last_stage(q, part) == age:
                     hand_on(side, q, part)
 
-    def image_step(q):
+    def join(q):
+        sibling(q).wait_recv()
+
+    def step(done, q):
         image_product(q)
+        text_product(done)
+        rank = RANK[q]
+        if rank:
+            grads(col_blocks(rank) + row_blocks(rank - 1))
         sibling(q).start()
-
-    def text_step(q):
-        if q:
-            grads(row_blocks(RANK[q] - 1) + col_blocks(RANK[q] - 1))
-        text_product(q)
-        rounds(1, (q,), 0)
-
-    def join(q):
-        join_cores(q)
-        rounds(0, (q,), 0)
-
+        rounds(1, (done,), 0)
+        join(done)
+        rounds(0, (done,), 0)
+
+    total_copy(0, 0).start()
     spread(7)
     grads(row_blocks(7))
-    image_step(7)
+    image_product(7)
     for rank in range(6, -1, -1):
         spread(rank)
-    grads(col_blocks(7))
-    text_step(7)
-    image_step(6)
-    join(7)
-    text_step(6)
-    image_step(3)
-    join(6)
-    text_step(3)
-    image_step(5)
-    join(3)
-    text_step(5)
+    grads(col_blocks(7) + row_blocks(6))
+    sibling(7).start()
+    taken(part_r, tot_recv.at[0])
+    part2_s[...] = part_s[...] + part_r[...]
+    for q in range(1, 8):
+        total_copy(1, q).start()
+    step(7, 6)
+    step(6, 3)
+    taken(part2_r, tot_recv.at[1])
+    part3_s[...] = functools.reduce(jnp.add, [part2_s[...]] + [part2_r[j] for j in range(7)])
+    for q in range(1, 8):
+        total_copy(2, q).start()
+    step(3, 5)
+    step(5, 4)
     rounds(1, (6, 3, 5), 1)
-    image_step(4)
-    join(5)
     rounds(0, (6, 3, 5), 1)
-    text_step(4)
-    image_step(2)
-    join(4)
-    text_step(2)
-    image_step(1)
-    join(2)
-    text_step(1)
-    for j in range(1, 16):
-        total_copy(0, j).start()
-    rounds(1, (4, 2, 1), 1)
-    image_step(0)
-    join(1)
-    rounds(0, (4, 2, 1), 1)
-    text_step(0)
+    step(4, 2)
+    step(2, 1)
+    rounds(1, (4,), 1)
+    rounds(0, (4,), 1)
+    step(1, 0)
+    rounds(1, (2, 1), 1)
+    rounds(0, (2, 1), 1)
+    text_product(0)
     rounds(1, (4, 2, 1), 2)
     rounds(0, (4, 2, 1), 2)
-    for j in range(1, 16):
-        total_copy(0, j).wait_recv()
-    part2_s[...] = functools.reduce(jnp.add, [part_s[...]] + [part_r[j] for j in range(15)])
-    for q in range(1, 8):
-        total_copy(1, q).start()
-    join_cores(0)
+    join(0)
 
     for side, out in ((1, text_out), (0, image_out)):
         for part in range(N_PARTS):
@@ -449,41 +453,19 @@
             g = out[here, :] * scale
             out[here, :] = inverse * (g - hat * jnp.sum(hat * g, axis=1, keepdims=True))
 
-    for q in range(1, 8):
-        total_copy(1, q).wait_recv()
-    totals = functools.reduce(jnp.add, [part2_s[...]] + [part2_r[j] for j in range(7)])
+    taken(part3_r, tot_recv.at[2])
+    totals = functools.reduce(jnp.add, [part3_s[...]] + [part3_r[j] for j in range(7)])
     pairs = 128.0 * CHUNK
-    sums_out[0] = jnp.sum(totals[0:8]) * (LN2 / (2.0 * pairs))
-    sums_out[1] = jnp.sum(totals[8:16]) * (LN2 / pairs)
-
-    for side in range(2):
-        for q in range(1, 8):
-            for part in range(N_PARTS):
-                gather_copy(side, q, part).wait_send()
-                sum_copy(side, q, part).wait_send()
-    for q in range(8):
-        sibling(q).wait_send()
-        for part in range(N_PARTS):
-            core_copy(q, part).wait_send()
-    for j in range(1, 16):
-        row_copy(j).wait_send()
-        total_copy(0, j).wait_send()
-    for q in range(1, 8):
-        col_copy(q).wait_send()
-        total_copy(1, q).wait_send()
-
-
-def deliver(image_ref, text_ref, sums_ref, loss_out, image_out, text_out, scale_out, sem):
-    copies = [
-        pltpu.make_async_copy(image_ref, image_out, sem.at[0]),
-        pltpu.make_async_copy(text_ref, text_out, sem.at[1]),
-    ]
-    for copy in copies:
-        copy.start()
-    loss_out[0] = sums_ref[0]
-    scale_out[0] = sums_ref[1]
-    for copy in copies:
-        copy.wait()
+    loss_out[0] = jnp.sum(totals[0:8]) * (LN2 / (2.0 * pairs))
+    scale_out[0] = jnp.sum(totals[8:16]) * (LN2 / pairs)
+
+    taken(rs_r.at[0], rs_send.at[0])
+    taken(rs_r.at[1], rs_send.at[1])
+    taken(core_s, core_send.at[1])
+    taken(part_r, tot_send.at[0])
+    taken(part2_r, tot_send.at[1])
+    taken(part3_r, tot_send.at[2])
+    gathered()
 
 
 def local(image_features, text_features, logit_scale):
@@ -491,15 +473,16 @@
     vmem = pl.BlockSpec(memory_space=pltpu.VMEM)
     smem = pl.BlockSpec(memory_space=pltpu.SMEM)
     dma = pltpu.SemaphoreType.DMA
-    image_grad, text_grad, sums = pl.pallas_call(
+    results = pl.pallas_call(
         kernel,
         out_shape=(
+            pltpu.SMEM((1,), F32),
             pltpu.VMEM((CHUNK, WIDTH), F32),
             pltpu.VMEM((CHUNK, WIDTH), F32),
-            pltpu.SMEM((2,), F32),
+            pltpu.SMEM((1,), F32),
         ),
         in_specs=[hbm] * 3,
-        out_specs=(vmem, vmem, smem),
+        out_specs=(smem, vmem, vmem, smem),
         scratch_shapes=[
             pltpu.SMEM((1,), F32),
             pltpu.VMEM((2, CHUNK, WIDTH), F32),
@@ -509,10 +492,11 @@
             pltpu.VMEM((1024, WIDTH), BF16),
             pltpu.VMEM((2048, 1024), F32),
             pltpu.VMEM((2048, 1024), BF16),
-            pltpu.VMEM((2048, 128), F32),
-            pltpu.VMEM((2048, 128), F32),
-            pltpu.VMEM((8, 1024), F32),
-            pltpu.VMEM((8, 1024), F32),
+            pltpu.VMEM((1024, 2048), BF16),
+            pltpu.VMEM((4, 2048, 128), F32),
+            pltpu.VMEM((4, 8, 1024), F32),
+            pltpu.VMEM((16, 128), F32),
+            pltpu.VMEM((8, 128), F32),
             pltpu.VMEM((16, 128), F32),
             pltpu.VMEM((15, 16, 128), F32),
             pltpu.VMEM((8, 128), F32),
@@ -527,38 +511,31 @@
             pltpu.VMEM((2, 1024, WIDTH), BF16),
             pltpu.VMEM((2, 7 * CHUNK, WIDTH), BF16),
             pltpu.VMEM((16, 128), F32),
-            pltpu.VMEM((15, 16, 128), F32),
+            pltpu.VMEM((16, 128), F32),
+            pltpu.VMEM((16, 128), F32),
+            pltpu.VMEM((7, 16, 128), F32),
             pltpu.VMEM((16, 128), F32),
             pltpu.VMEM((7, 16, 128), F32),
             dma((3,)),
+            dma((2,)),
             dma((2, 7 * N_PARTS)),
+            dma((2,)),
+            dma((16,)),
+            dma((1,)),
+            dma((1,)),
+            dma((1,)),
+            dma((1,)),
+            dma((2,)),
             dma((2, 7 * N_PARTS)),
-            dma((8 * N_PARTS + 8,)),
-            dma((8 * N_PARTS + 8,)),
-            dma((15,)),
-            dma((15,)),
-            dma((7,)),
-            dma((7,)),
-            dma((2, 7 * N_PARTS)),
-            dma((2, 7 * N_PARTS)),
-            dma((22,)),
-            dma((22,)),
+            dma((3,)),
+            dma((3,)),
         ],
         compiler_params=pltpu.CompilerParams(
             collective_id=0, has_side_effects=True, vmem_limit_bytes=60 * 2**20
         ),
         name="contrastive",
     )(logit_scale, image_features, text_features)
-    one = jax.ShapeDtypeStruct((1,), F32)
-    grad = jax.ShapeDtypeStruct((CHUNK, WIDTH), F32)
-    return pl.pallas_call(
-        deliver,
-        out_shape=(one, grad, grad, one),
-        in_specs=[vmem, vmem, smem],
-        out_specs=(smem, hbm, hbm, smem),
-        scratch_shapes=[dma((2,))],
-        name="finish",
-    )(image_grad, text_grad, sums)
+    return results
 
 
 def solution(mesh):

time: 67.9 us -> 62.9 us (0.926)
  Pallas kernels: 64.7 us -> 58.4 us
  between operations: 1.48 us -> 2.32 us
    pallas_call x2 -> x1, Pallas kernels: 64.7 us -> 58.4 us  [local(): pl.pallas_call(kernel, out_shape=(pltpu.SMEM((1,), F32), pltpu.VMEM((CHUN...]
    unnamed x4 -> x2, local copies, waits for them, and re-layouts: 1.58 us -> 1.59 us
where the time goes in v3:
time: 62.9 us; the launch traced here: 62.3 us
  Pallas kernels  58.4 us (93%)
  between operations  2.32 us (4%)
  local copies, waits for them, and re-layouts  1.59 us (3%)
    pallas_call x1, Pallas kernels, local(): pl.pallas_call(kernel, out_shape=(pltpu.SMEM((1,), F32), pltpu.VMEM((CHUN...  58.4 us
    unnamed x2, local copies, waits for them, and re-layouts  1.59 us

profile of v3, /device:TPU:1, one launch (start us, length us, event | category | flops | bytes accessed | tf_op | source)
XLA Modules:
  0.0 62.3 jit_solution(2260993305318089786)
XLA Ops:
  1.3 58.4 %contrastive.1 = (f32[1]{0:T(128)S(4)}, f32[128,1024]{1,0:T(8,128)S(1)}, f32[128,1024]{1,0:T(8,128)S(1)}, f32[1]{0:T(128)S(4)}) custom-call(f32[1]{0:T(128)S(6)} %copy.15.scale_ref, f32[128,1024]{1,0:T(8,128)} %image_ref.1, f32[128,1024]{1,0:T(8,128)} %text_ref.1), custom_call_target="tpu_custom_call" | custom-call | tf_op jit(solution)/shard_map/contrastive/pallas_call | solution.py:476
  60.7 0.8 %copy.12 = f32[128,1024]{1,0:T(8,128)} copy(f32[128,1024]{1,0:T(8,128)S(1)} %get-tuple-element.5) | data formatting | bytes 1048576
  61.5 0.8 %copy.13 = f32[128,1024]{1,0:T(8,128)} copy(f32[128,1024]{1,0:T(8,128)S(1)} %get-tuple-element.6) | data formatting | bytes 1048576

commit v4 on v3

--- a/solution.py
+++ b/solution.py
@@ -64,7 +64,7 @@
     scale_ref, image_ref, text_ref,
     loss_out, image_out, text_out, scale_out,
     scale_s, feat_s, lse_s, eye_s,
-    img, txt, u_s, grad_s, flip_s, row_acc, col_acc, rowm_s, colm_s,
+    img, txt, u_s, grad_s, flip_s, row_acc, col_acc, rows_s, cols_s,
     rowl_s, rowl_r, coll_s, coll_r, rlse_s, clse_s, crow_s,
     a_img, a_txt, core_s, core_r, rs_s, rs_r,
     part_s, part_r, part2_s, part2_r, part3_s, part3_r,
@@ -195,13 +195,17 @@
     def row_index(q, other):
         return absolute(0, q) * 2 + (1 - k if other else k)
 
-    def row_sums(q):
+    def row_sums(q, kinds):
         for other in range(2):
-            r = RANK[q] * 256 + other * CHUNK
-            sums = [jnp.sum(row_acc[i, pl.ds(r, CHUNK), :].T, axis=0, keepdims=True) for i in range(4)]
-            here = pl.ds(row_index(q, other), 1)
-            rowl_s[here, :] = joined(*sums[:2])
-            rowm_s[here, :] = averaged(*sums)
+            for i in kinds:
+                row = row_acc[i, pl.ds(RANK[q] * 256 + other * CHUNK, CHUNK), :]
+                rows_s[i, pl.ds(row_index(q, other), 1), :] = jnp.sum(row.T, axis=0, keepdims=True)
+
+    def col_sums(kinds):
+        for i in kinds:
+            row = jnp.sum(col_acc[i], axis=0, keepdims=True)
+            for q in range(8):
+                cols_s[i, pl.ds(absolute(1, q), 1), :] = row[:, RANK[q] * 128 : (RANK[q] + 1) * 128]
 
     arrive(1, 0, 1, 2)
     arrive(4, 2, 0)
@@ -244,19 +248,10 @@
 
     scores(0, 1792, 896, 128)
     for q in ORDER[:7]:
-        row_sums(q)
+        row_sums(q, (0, 1))
     both_cores(7)
     scores(1792, 256, 0, 512)
     scores(1792, 256, 512, 512)
-
-    row_sums(7)
-    sums = [jnp.sum(col_acc[i], axis=0, keepdims=True) for i in range(4)]
-    col_lse, col_mean = joined(*sums[:2]), averaged(*sums)
-    for q in range(8):
-        here, at_col = pl.ds(absolute(1, q), 1), slice(RANK[q] * 128, (RANK[q] + 1) * 128)
-        coll_s[here, :] = col_lse[:, at_col]
-        colm_s[here, :] = col_mean[:, at_col]
-    part_s[...] = jnp.zeros_like(part_s)
 
     def matching(q, other):
         ix, iy, iz = (flipped[0][d] if q >> d & 1 else at[d] for d in range(3))
@@ -271,7 +266,6 @@
         rank = sum(jnp.where(slot == q, RANK[q], 0) for q in range(1, 8))
         return jnp.where(here, rank, -1)
 
-    matches = [matching(q, other) for q in ORDER for other in range(2)]
 
     def row_copy(j):
         return remote(rowl_s, rowl_r.at[j - 1], lse_send.at[0], lse_recv.at[0], place(0, j >> 1, j & 1))
@@ -279,10 +273,19 @@
     def col_copy(q):
         return remote(coll_s, coll_r.at[q - 1], csum_send.at[0], csum_recv.at[0], place(1, q))
 
-    for q in range(1, 8):
+    col_sums((0, 1))
+    coll_s[...] = joined(cols_s[0], cols_s[1])
+    for q in (7, 3, 5, 6, 1, 2, 4):
         col_copy(q).start()
-    for j in range(1, 16):
+    row_sums(7, (0, 1))
+    rowl_s[...] = joined(rows_s[0], rows_s[1])
+    for j in (15, 14, 13, 12, 11, 10, 7, 6, 9, 8, 5, 4, 3, 2, 1):
         row_copy(j).start()
+    part_s[...] = jnp.zeros_like(part_s)
+    col_sums((2, 3))
+    for q in range(8):
+        row_sums(q, (2, 3))
+    matches = [matching(q, other) for q in ORDER for other in range(2)]
     for i, rank in enumerate(matches):
 
         @pl.when(rank >= 0)
@@ -323,8 +326,8 @@
                 grad_s[here, at_col] = low
                 flip_s[at_col, here] = low.T
 
-    weighted = jnp.exp2(rowl_s[...] - rlse_s[...]) * rowm_s[...]
-    weighted = weighted[0:8] + weighted[8:16] + jnp.exp2(coll_s[...] - clse_s[...]) * colm_s[...]
+    weighted = jnp.exp2(rowl_s[...] - rlse_s[...]) * averaged(*(rows_s[i] for i in range(4)))
+    weighted = weighted[0:8] + weighted[8:16] + jnp.exp2(coll_s[...] - clse_s[...]) * averaged(*(cols_s[i] for i in range(4)))
     part_s[pl.ds(8, 8), :] += 0.5 * weighted
     part_s[pl.ds(0, 1), :] += rlse_s[pl.ds(row_index(0, 0), 1), :] + clse_s[pl.ds(absolute(1, 0), 1), :]
 
@@ -408,34 +411,73 @@
         join(done)
         rounds(0, (done,), 0)
 
+    def totals_1():
+        taken(part_r, tot_recv.at[0])
+        part2_s[...] = part_s[...] + part_r[...]
+        for q in range(1, 8):
+            total_copy(1, q).start()
+
+    def totals_2():
+        taken(part2_r, tot_recv.at[1])
+        part3_s[...] = functools.reduce(jnp.add, [part2_s[...]] + [part2_r[j] for j in range(7)])
+        for q in range(1, 8):
+            total_copy(2, q).start()
+
+    def corner(rank):
+        grads(row_blocks(rank) + col_blocks(rank))
+
+    def image_turn(q):
+        image_product(q)
+        sibling(q).start()
+
+    def text_turn(q):
+        text_product(q)
+        rounds(1, (q,), 0)
+
+    def join_turn(q):
+        join(q)
+        rounds(0, (q,), 0)
+
     total_copy(0, 0).start()
-    spread(7)
-    grads(row_blocks(7))
-    image_product(7)
-    for rank in range(6, -1, -1):
+    for rank in range(7, -1, -1):
         spread(rank)
-    grads(col_blocks(7) + row_blocks(6))
-    sibling(7).start()
-    taken(part_r, tot_recv.at[0])
-    part2_s[...] = part_s[...] + part_r[...]
-    for q in range(1, 8):
-        total_copy(1, q).start()
-    step(7, 6)
-    step(6, 3)
-    taken(part2_r, tot_recv.at[1])
-    part3_s[...] = functools.reduce(jnp.add, [part2_s[...]] + [part2_r[j] for j in range(7)])
-    for q in range(1, 8):
-        total_copy(2, q).start()
-    step(3, 5)
-    step(5, 4)
+    corner(7)
+    image_turn(7)
+    text_turn(7)
+    corner(6)
+    image_turn(6)
+    join_turn(7)
+    text_turn(6)
+    totals_1()
+    corner(5)
+    image_turn(3)
+    join_turn(6)
+    text_turn(3)
+    corner(4)
+    image_turn(5)
+    join_turn(3)
+    text_turn(5)
+    totals_2()
     rounds(1, (6, 3, 5), 1)
+    corner(3)
+    image_turn(4)
+    join_turn(5)
     rounds(0, (6, 3, 5), 1)
-    step(4, 2)
-    step(2, 1)
+    text_turn(4)
+    corner(2)
+    image_turn(2)
+    join_turn(4)
+    text_turn(2)
     rounds(1, (4,), 1)
+    corner(1)
+    corner(0)
+    image_turn(1)
+    join_turn(2)
     rounds(0, (4,), 1)
-    step(1, 0)
+    text_turn(1)
     rounds(1, (2, 1), 1)
+    image_turn(0)
+    join_turn(1)
     rounds(0, (2, 1), 1)
     text_product(0)
     rounds(1, (4, 2, 1), 2)
@@ -495,8 +537,8 @@
             pltpu.VMEM((1024, 2048), BF16),
             pltpu.VMEM((4, 2048, 128), F32),
             pltpu.VMEM((4, 8, 1024), F32),
-            pltpu.VMEM((16, 128), F32),
-            pltpu.VMEM((8, 128), F32),
+            pltpu.VMEM((4, 16, 128), F32),
+            pltpu.VMEM((4, 8, 128), F32),
             pltpu.VMEM((16, 128), F32),
             pltpu.VMEM((15, 16, 128), F32),
             pltpu.VMEM((8, 128), F32),

time: 62.9 us -> 61.9 us (0.984)
  no operation moved by 1% of the time
where the time goes in v4:
time: 61.9 us; the launch traced here: 61.7 us
  Pallas kernels  57.8 us (93%)
  between operations  2.32 us (4%)
  local copies, waits for them, and re-layouts  1.59 us (3%)
    pallas_call x1, Pallas kernels, local(): pl.pallas_call(kernel, out_shape=(pltpu.SMEM((1,), F32), pltpu.VMEM((CHUN...  57.8 us
    unnamed x2, local copies, waits for them, and re-layouts  1.59 us

profile of v4, /device:TPU:1, one launch (start us, length us, event | category | flops | bytes accessed | tf_op | source)
XLA Modules:
  0.0 61.7 jit_solution(16238219970004940666)
XLA Ops:
  1.3 57.8 %contrastive.1 = (f32[1]{0:T(128)S(4)}, f32[128,1024]{1,0:T(8,128)S(1)}, f32[128,1024]{1,0:T(8,128)S(1)}, f32[1]{0:T(128)S(4)}) custom-call(f32[1]{0:T(128)S(6)} %copy.15.scale_ref, f32[128,1024]{1,0:T(8,128)} %image_ref.1, f32[128,1024]{1,0:T(8,128)} %text_ref.1), custom_call_target="tpu_custom_call" | custom-call | tf_op jit(solution)/shard_map/contrastive/pallas_call | solution.py:518
  60.2 0.8 %copy.12 = f32[128,1024]{1,0:T(8,128)} copy(f32[128,1024]{1,0:T(8,128)S(1)} %get-tuple-element.5) | data formatting | bytes 1048576
  61.0 0.8 %copy.13 = f32[128,1024]{1,0:T(8,128)} copy(f32[128,1024]{1,0:T(8,128)S(1)} %get-tuple-element.6) | data formatting | bytes 1048576

commit v5 on v4

--- a/solution.py
+++ b/solution.py
@@ -63,7 +63,7 @@
 def kernel(
     scale_ref, image_ref, text_ref,
     loss_out, image_out, text_out, scale_out,
-    scale_s, feat_s, lse_s, eye_s,
+    scale_s, feat_s, inv_s, lse_s, eye_s,
     img, txt, u_s, grad_s, flip_s, row_acc, col_acc, rows_s, cols_s,
     rowl_s, rowl_r, coll_s, coll_r, rlse_s, clse_s, crow_s,
     a_img, a_txt, core_s, core_r, rs_s, rs_r,
@@ -109,15 +109,6 @@
     img[pl.ds(0, CHUNK), :] = normalized(0).astype(BF16)
     loads[1].wait()
     txt[pl.ds(0, CHUNK), :] = normalized(1).astype(BF16)
-    loads[2].wait()
-    scale = jnp.exp(jnp.full((8, 128), scale_s[0], F32))[0:1, 0:1]
-    unit = scale * LOG2E
-    row_acc[...] = jnp.zeros_like(row_acc)
-    col_acc[...] = jnp.zeros_like(col_acc)
-
-    eye = lax.broadcasted_iota(jnp.int32, (CHUNK, CHUNK), 0) == lax.broadcasted_iota(jnp.int32, (CHUNK, CHUNK), 1)
-    eye_s[pl.ds(0, CHUNK), :] = jnp.zeros((CHUNK, CHUNK), F32)
-    eye_s[pl.ds(CHUNK, CHUNK), :] = jnp.where(eye, 1.0, 0.0)
     pl.semaphore_wait(barrier, len(peers))
 
     def area(part, base):
@@ -149,7 +140,8 @@
                     gather_copy(side, q, part).wait_recv()
                     for d in dims:
                         gather_copy(side, q | 1 << d, part).start()
-                core_copy(q, part).start()
+                    if side == 0:
+                        core_copy(q, part).start()
 
     def send_on(q, first):
         for part in range(N_PARTS):
@@ -167,6 +159,21 @@
             send_on(1 << d, (d - t) % 3)
     for part in range(N_PARTS):
         core_copy(0, part).start()
+
+    loads[2].wait()
+    scale = jnp.exp(jnp.full((8, 128), scale_s[0], F32))[0:1, 0:1]
+    unit = scale * LOG2E
+    row_acc[...] = jnp.zeros_like(row_acc)
+    col_acc[...] = jnp.zeros_like(col_acc)
+
+    eye = lax.broadcasted_iota(jnp.int32, (CHUNK, CHUNK), 0) == lax.broadcasted_iota(jnp.int32, (CHUNK, CHUNK), 1)
+    eye_s[pl.ds(0, CHUNK), :] = jnp.zeros((CHUNK, CHUNK), F32)
+    eye_s[pl.ds(CHUNK, CHUNK), :] = jnp.where(eye, 1.0, 0.0)
+    for side in range(2):
+        v = feat_s[side]
+        inverse = lax.rsqrt(jnp.sum(v * v, axis=1, keepdims=True) + EPS)
+        feat_s[side] = v * inverse
+        inv_s[side] = jnp.broadcast_to(inverse, (CHUNK, 128))
 
     def scores(row0, rows, col0, cols):
         for r in range(row0, row0 + rows, 256):
@@ -376,19 +383,21 @@
             rs_send.at[side], rs_recv.at[side, i], place(side, 1 << d),
         )
 
-    def summed(side, q, part):
+    def received(side, q, part, stage):
+        sum_copy(side, q | 1 << stage_dim(part, stage), part).wait_recv()
+        return rs_r[(side, *area(part, region(q, part, stage) * CHUNK))].astype(F32)
+
+    def summed(side, q, part, upto):
         acc = (a_img, a_txt)[side][area(part, RANK[q] * CHUNK)]
         if side == 0:
             acc = acc + core_r[area(part, q * CHUNK)].astype(F32)
-        for stage in range(2, last_stage(q, part), -1):
-            d = stage_dim(part, stage)
-            sum_copy(side, q | 1 << d, part).wait_recv()
-            acc = acc + rs_r[(side, *area(part, region(q, part, stage) * CHUNK))].astype(F32)
+        for stage in range(2, upto, -1):
+            acc = acc + received(side, q, part, stage)
         return acc
 
     def hand_on(side, q, part):
         if not (side == 1 and last_stage(q, part) == 2):
-            rs_s[(side, *area(part, q * CHUNK))] = summed(side, q, part).astype(BF16)
+            rs_s[(side, *area(part, q * CHUNK))] = summed(side, q, part, last_stage(q, part)).astype(BF16)
         sum_copy(side, q, part).start()
 
     def rounds(side, slots, age):
@@ -484,16 +493,16 @@
     rounds(0, (4, 2, 1), 2)
     join(0)
 
-    for side, out in ((1, text_out), (0, image_out)):
+    outs = (image_out, text_out)
+    for side in (1, 0):
         for part in range(N_PARTS):
-            out[area(part, 0)] = summed(side, 0, part)
-        for row in range(0, CHUNK, 32):
-            here = pl.ds(row, 32)
-            v = feat_s[side, here, :]
-            inverse = lax.rsqrt(jnp.sum(v * v, axis=1, keepdims=True) + EPS)
-            hat = v * inverse
-            g = out[here, :] * scale
-            out[here, :] = inverse * (g - hat * jnp.sum(hat * g, axis=1, keepdims=True))
+            outs[side][area(part, 0)] = summed(side, 0, part, 0)
+    for side in (1, 0):
+        for part in range(N_PARTS):
+            outs[side][area(part, 0)] += received(side, 0, part, 0)
+        hat, g = feat_s[side], outs[side][...] * scale
+        inverse = inv_s[side][:, 0:1]
+        outs[side][...] = inverse * (g - hat * jnp.sum(hat * g, axis=1, keepdims=True))
 
     taken(part3_r, tot_recv.at[2])
     totals = functools.reduce(jnp.add, [part3_s[...]] + [part3_r[j] for j in range(7)])
@@ -528,6 +537,7 @@
         scratch_shapes=[
             pltpu.SMEM((1,), F32),
             pltpu.VMEM((2, CHUNK, WIDTH), F32),
+            pltpu.VMEM((2, CHUNK, 128), F32),
             pltpu.VMEM((2048, 128), F32),
             pltpu.VMEM((2 * CHUNK, CHUNK), F32),
             pltpu.VMEM((2048, WIDTH), BF16),

time: 61.9 us -> 61.5 us (level)
  no operation moved by 1% of the time
where the time goes in v5:
time: 61.5 us; the launch traced here: 61.3 us
  Pallas kernels  57.4 us (93%)
  between operations  2.32 us (4%)
  local copies, waits for them, and re-layouts  1.59 us (3%)
    pallas_call x1, Pallas kernels, local(): pl.pallas_call(kernel, out_shape=(pltpu.SMEM((1,), F32), pltpu.VMEM((CHUN...  57.4 us
    unnamed x2, local copies, waits for them, and re-layouts  1.59 us

profile of v5, /device:TPU:1, one launch (start us, length us, event | category | flops | bytes accessed | tf_op | source)
XLA Modules:
  0.0 61.3 jit_solution(10789032315421165612)
XLA Ops:
  1.3 57.4 %contrastive.1 = (f32[1]{0:T(128)S(4)}, f32[128,1024]{1,0:T(8,128)S(1)}, f32[128,1024]{1,0:T(8,128)S(1)}, f32[1]{0:T(128)S(4)}) custom-call(f32[1]{0:T(128)S(6)} %copy.15.scale_ref, f32[128,1024]{1,0:T(8,128)} %image_ref.1, f32[128,1024]{1,0:T(8,128)} %text_ref.1), custom_call_target="tpu_custom_call" | custom-call | tf_op jit(solution)/shard_map/contrastive/pallas_call | solution.py:527
  59.7 0.8 %copy.12 = f32[128,1024]{1,0:T(8,128)} copy(f32[128,1024]{1,0:T(8,128)S(1)} %get-tuple-element.5) | data formatting | bytes 1048576
  60.5 0.8 %copy.13 = f32[128,1024]{1,0:T(8,128)} copy(f32[128,1024]{1,0:T(8,128)S(1)} %get-tuple-element.6) | data formatting | bytes 1048576

commit v6 on v5

--- a/solution.py
+++ b/solution.py
@@ -254,10 +254,10 @@
         taken(coll_r, csum_send.at[0])
 
     scores(0, 1792, 896, 128)
+    both_cores(7)
+    scores(1792, 256, 0, 512)
     for q in ORDER[:7]:
         row_sums(q, (0, 1))
-    both_cores(7)
-    scores(1792, 256, 0, 512)
     scores(1792, 256, 512, 512)
 
     def matching(q, other):

time: 61.5 us -> 61.5 us (level)
  no operation moved by 1% of the time
where the time goes in v6:
time: 61.5 us; the launch traced here: 61.3 us
  Pallas kernels  57.4 us (93%)
  between operations  2.32 us (4%)
  local copies, waits for them, and re-layouts  1.59 us (3%)
    pallas_call x1, Pallas kernels, local(): pl.pallas_call(kernel, out_shape=(pltpu.SMEM((1,), F32), pltpu.VMEM((CHUN...  57.4 us
    unnamed x2, local copies, waits for them, and re-layouts  1.59 us

profile of v6, /device:TPU:1, one launch (start us, length us, event | category | flops | bytes accessed | tf_op | source)
XLA Modules:
  0.0 61.3 jit_solution(10301839435957752961)
XLA Ops:
  1.3 57.4 %contrastive.1 = (f32[1]{0:T(128)S(4)}, f32[128,1024]{1,0:T(8,128)S(1)}, f32[128,1024]{1,0:T(8,128)S(1)}, f32[1]{0:T(128)S(4)}) custom-call(f32[1]{0:T(128)S(6)} %copy.15.scale_ref, f32[128,1024]{1,0:T(8,128)} %image_ref.1, f32[128,1024]{1,0:T(8,128)} %text_ref.1), custom_call_target="tpu_custom_call" | custom-call | tf_op jit(solution)/shard_map/contrastive/pallas_call | solution.py:527
  59.8 0.8 %copy.12 = f32[128,1024]{1,0:T(8,128)} copy(f32[128,1024]{1,0:T(8,128)S(1)} %get-tuple-element.5) | data formatting | bytes 1048576
  60.5 0.8 %copy.13 = f32[128,1024]{1,0:T(8,128)} copy(f32[128,1024]{1,0:T(8,128)S(1)} %get-tuple-element.6) | data formatting | bytes 1048576
